TPU v7x, 32 devices: a whole 2x2x4 slice. The times are simulated.
32 devices in a mesh: dp: 2 (over core), fsdp: 16 (over z, y, x).
Axes of the slice: x: 2, y: 2, z: 4, core: 2. Of those that a mesh axis runs over, the one named last changes fastest.
Arguments:
- images: bfloat16 [256, 256, 256], P(('dp', 'fsdp')), may hold values from -6 to 6
- timesteps: int32 [256], P(('dp', 'fsdp')), may hold values from 0 to 999
- labels: int32 [256], P(('dp', 'fsdp')), may hold values from 0 to 9
- valid_slot: int32 [256], P(('dp', 'fsdp')), may hold values from 0 to 1
- noise_idx: int32 [256, 256], P(('dp', 'fsdp')), may hold values from 0 to 255
- noise_table: float32 [256, 256], replicated, may hold values from -6 to 6
- params_a: float32 [1646592], P('fsdp')
- params_b: float32 [329728], P('fsdp')
- first_a: float32 [1646592], P('fsdp')
- second_a: float32 [1646592], P('fsdp')
- first_b: float32 [329728], P('fsdp')
- second_b: float32 [329728], P('fsdp')
Outputs:
- new_a: float32 [1646592], P('fsdp')
- moment_one_a: float32 [1646592], P('fsdp')
- moment_two_a: float32 [1646592], P('fsdp')
- copy_a: bfloat16 [1646592], P('fsdp')
- new_b: float32 [329728], P('fsdp')
- moment_one_b: float32 [329728], P('fsdp')
- moment_two_b: float32 [329728], P('fsdp')
- copy_b: bfloat16 [329728], P('fsdp')
- loss_sum: float32 [], replicated
- pixel_count: float32 [], replicated
- grad_norm: float32 [], replicated
All inputs are finite; a program needn't handle non-finite values.
Results may differ from a plain program's by a relative error of at most 0.012.
Values may be sent and summed in bfloat16 or wider, within the bound.
A program may use at most 192 MiB of HBM per device.

v0:
```python
import math

import jax
import jax.numpy as jnp
from jax import lax
from jax.sharding import PartitionSpec as P

C = 256
GROUPS = 32
SIDE = 16
POS = 256
TE = 512
SIN = 128
NCLS = 10
NT = 256
STEP = 5
PA = 1646592
PB = 329728


eps_norm = 1e-05
beta_one = 0.5
beta_two = 0.5
learn_rate = 0.1
decay_rate = 0.01
adam_eps = 1e-08
clip_level = 0.01
highest = lax.Precision.HIGHEST


def first_shapes():
    return [
        (2, C),
        (9 * C, C),
        (C,),
        (SIN, TE),
        (TE,),
        (TE, TE),
        (TE,),
        (NCLS, TE),
        (TE, C),
        (C,),
        (2, C),
        (9 * C, C),
        (C,),
    ]


def second_shapes():
    return [(2, C), (C, 3 * C), (2 * C,), (C, C), (C,), (2, C), (C, C), (C,)]


def unpack(vector, shapes):
    result = []
    offset = 0
    for extent in shapes:
        length = math.prod(extent)
        result.append(vector[offset : offset + length].reshape(extent))
        offset += length
    return result


def flatten(pieces, total_len):
    joined = jnp.concatenate([p.reshape(-1) for p in pieces])
    return jnp.concatenate([joined, jnp.zeros((total_len - joined.shape[0],), jnp.float32)])


def fetch_weights(vector):
    return lax.all_gather(vector.astype(jnp.bfloat16), "fsdp", axis=0, tiled=True)


def refetch_weights(vector):
    return lax.all_gather(vector.astype(jnp.bfloat16), "fsdp", axis=0, tiled=True)


def swish(v):
    return v * jax.nn.sigmoid(v)


def swish_grad(v):
    sigmoid_v = jax.nn.sigmoid(v)
    return sigmoid_v * (1.0 + v * (1.0 - sigmoid_v))


def small_dot(a, b):
    return jnp.dot(a, b.astype(jnp.float32), precision=highest, preferred_element_type=jnp.float32)


def sinusoid(steps_in):
    half_dim = SIN // 2
    factor = math.log(10000.0) / (half_dim - 1)
    frequency = jnp.exp(jnp.arange(half_dim, dtype=jnp.float32) * -factor)
    angles = steps_in.astype(jnp.float32)[:, None] * frequency[None, :]
    return jnp.concatenate([jnp.sin(angles), jnp.cos(angles)], axis=1)


def norm_forward(values, gain_bias):
    gb_f = gain_bias.astype(jnp.float32)
    grouped = values.reshape(values.shape[0], values.shape[1], GROUPS, C // GROUPS)
    centre = grouped - jnp.mean(grouped, axis=(1, 3), keepdims=True)
    spread = jnp.mean(centre * centre, axis=(1, 3), keepdims=True)
    inv_std = lax.rsqrt(spread + eps_norm)
    scaled = centre * inv_std
    return (scaled.reshape(values.shape) * gb_f[0] + gb_f[1], (scaled, inv_std))


def norm_backward(d_out, gain_bias, kept_norm):
    scaled, inv_std = kept_norm
    flat_scaled = scaled.reshape(d_out.shape)
    d_gains = jnp.sum(d_out * flat_scaled, axis=(0, 1))
    d_biases = jnp.sum(d_out, axis=(0, 1))
    d_scaled = (d_out * gain_bias[0].astype(jnp.float32)).reshape(scaled.shape)
    d_in = inv_std * (
        d_scaled
        - jnp.mean(d_scaled, axis=(1, 3), keepdims=True)
        - scaled * jnp.mean(d_scaled * scaled, axis=(1, 3), keepdims=True)
    )
    return (d_in.reshape(d_out.shape), jnp.stack([d_gains, d_biases]))


def columns_of(values):
    count_img = values.shape[0]
    planes = values.reshape(count_img, SIDE, SIDE, C)
    padded = jnp.pad(planes, ((0, 0), (1, 1), (1, 1), (0, 0)))
    columns = jnp.concatenate(
        [padded[:, r : r + SIDE, s : s + SIDE, :] for r in range(3) for s in range(3)], axis=3
    )
    return columns.reshape(count_img * POS, 9 * C)


def conv_apply(columns, kernel):
    output = jnp.dot(columns, kernel, preferred_element_type=jnp.float32)
    return output.reshape(columns.shape[0] // POS, POS, C)


def conv_backward(d_out, columns, kernel):
    count_img = d_out.shape[0]
    d_low = d_out.astype(jnp.bfloat16).reshape(count_img * POS, C)
    d_kernel = lax.dot_general(
        columns, d_low, (((0,), (0,)), ((), ())), preferred_element_type=jnp.float32
    )
    d_cols = lax.dot_general(
        d_low, kernel, (((1,), (1,)), ((), ())), preferred_element_type=jnp.float32
    )
    d_cols = d_cols.reshape(count_img, SIDE, SIDE, 9, C)
    d_padded = jnp.zeros((count_img, SIDE + 2, SIDE + 2, C), jnp.float32)
    for r in range(3):
        for s in range(3):
            d_padded = d_padded.at[:, r : r + SIDE, s : s + SIDE, :].add(
                d_cols[:, :, :, r * 3 + s, :]
            )
    return (d_padded[:, 1 : SIDE + 1, 1 : SIDE + 1, :].reshape(count_img, POS, C), d_kernel)


def forward_first(w_a, h_zero, steps_in, classes):
    (
        norm_one,
        kernel_one,
        bias_one,
        time_w1,
        time_b1,
        time_w2,
        time_b2,
        class_table,
        proj_time,
        proj_bias,
        norm_two,
        kernel_two,
        bias_two,
    ) = w_a
    embedding = sinusoid(steps_in)
    pre_one = small_dot(embedding, time_w1) + time_b1.astype(jnp.float32)
    hidden_one = swish(pre_one)
    onehot_cls = (classes[:, None] == jnp.arange(NCLS, dtype=jnp.int32)[None, :]).astype(
        jnp.float32
    )
    time_embed = (
        small_dot(hidden_one, time_w2)
        + time_b2.astype(jnp.float32)
        + small_dot(onehot_cls, class_table)
    )
    time_act = swish(time_embed)
    time_add = small_dot(time_act, proj_time) + proj_bias.astype(jnp.float32)
    a_one, keep_one = norm_forward(h_zero, norm_one)
    cols_one = columns_of(swish(a_one).astype(jnp.bfloat16))
    c_one = conv_apply(cols_one, kernel_one) + bias_one.astype(jnp.float32) + time_add[:, None, :]
    a_two, keep_two = norm_forward(c_one, norm_two)
    cols_two = columns_of(swish(a_two).astype(jnp.bfloat16))
    h_one = h_zero + conv_apply(cols_two, kernel_two) + bias_two.astype(jnp.float32)
    kept_a = (
        embedding,
        pre_one,
        hidden_one,
        onehot_cls,
        time_embed,
        time_act,
        a_one,
        keep_one,
        cols_one,
        a_two,
        keep_two,
        cols_two,
    )
    return (h_one, kept_a)


def backward_first(w_a, kept_a, d_h_one):
    (
        norm_one,
        kernel_one,
        bias_one,
        time_w1,
        time_b1,
        time_w2,
        time_b2,
        class_table,
        proj_time,
        proj_bias,
        norm_two,
        kernel_two,
        bias_two,
    ) = w_a
    (
        embedding,
        pre_one,
        hidden_one,
        onehot_cls,
        time_embed,
        time_act,
        a_one,
        keep_one,
        cols_one,
        a_two,
        keep_two,
        cols_two,
    ) = kept_a
    d_bias_two = jnp.sum(d_h_one, axis=(0, 1))
    d_x_two, d_kernel_two = conv_backward(d_h_one, cols_two, kernel_two)
    d_c_one, d_norm_two = norm_backward(d_x_two * swish_grad(a_two), norm_two, keep_two)
    d_bias_one = jnp.sum(d_c_one, axis=(0, 1))
    d_time_add = jnp.sum(d_c_one, axis=1)
    d_x_one, d_kernel_one = conv_backward(d_c_one, cols_one, kernel_one)
    _, d_norm_one = norm_backward(d_x_one * swish_grad(a_one), norm_one, keep_one)
    d_proj_bias = jnp.sum(d_time_add, axis=0)
    d_proj_time = small_dot(time_act.T, d_time_add)
    d_time_embed = small_dot(d_time_add, proj_time.T) * swish_grad(time_embed)
    d_class_table = small_dot(onehot_cls.T, d_time_embed)
    d_time_b2 = jnp.sum(d_time_embed, axis=0)
    d_time_w2 = small_dot(hidden_one.T, d_time_embed)
    d_pre_one = small_dot(d_time_embed, time_w2.T) * swish_grad(pre_one)
    d_time_w1 = small_dot(embedding.T, d_pre_one)
    d_time_b1 = jnp.sum(d_pre_one, axis=0)
    return [
        d_norm_one,
        d_kernel_one,
        d_bias_one,
        d_time_w1,
        d_time_b1,
        d_time_w2,
        d_time_b2,
        d_class_table,
        d_proj_time,
        d_proj_bias,
        d_norm_two,
        d_kernel_two,
        d_bias_two,
    ]


def split_triple(triple):
    return (triple[..., :C], triple[..., C : 2 * C], triple[..., 2 * C :])


def attn_scores(queries, attn_keys):
    return jnp.einsum(
        "npc,nqc->npq", queries, attn_keys, preferred_element_type=jnp.float32
    ) * C ** (-0.5)


def forward_second(w_b, h_one):
    norm_three, triple_weight, qv_bias, out_weight, out_bias, norm_four, head_weight, head_bias = (
        w_b
    )
    a_three, keep_three = norm_forward(h_one, norm_three)
    x_three = a_three.astype(jnp.bfloat16)
    qv_f = qv_bias.astype(jnp.float32)
    bias_all = jnp.concatenate([qv_f[:C], jnp.zeros((C,), jnp.float32), qv_f[C:]])
    triple = (
        jnp.einsum("npc,cd->npd", x_three, triple_weight, preferred_element_type=jnp.float32)
        + bias_all
    ).astype(jnp.bfloat16)
    queries, attn_keys, attn_values = split_triple(triple)
    scores = attn_scores(queries, attn_keys)
    row_peak = jnp.max(scores, axis=2, keepdims=True)
    log_total = row_peak + jnp.log(jnp.sum(jnp.exp(scores - row_peak), axis=2, keepdims=True))
    attn_probs = jnp.exp(scores - log_total).astype(jnp.bfloat16)
    attn_mixed = jnp.einsum(
        "npq,nqc->npc", attn_probs, attn_values, preferred_element_type=jnp.float32
    ).astype(jnp.bfloat16)
    h_two = (
        h_one
        + jnp.einsum("npc,cd->npd", attn_mixed, out_weight, preferred_element_type=jnp.float32)
        + out_bias.astype(jnp.float32)
    )
    a_four, keep_four = norm_forward(h_two, norm_four)
    x_four = swish(a_four).astype(jnp.bfloat16)
    predict = jnp.einsum(
        "npc,cd->npd", x_four, head_weight, preferred_element_type=jnp.float32
    ) + head_bias.astype(jnp.float32)
    kept_b = (keep_three, x_three, triple, log_total, attn_mixed, a_four, keep_four, x_four)
    return (predict, kept_b)


def backward_second(w_b, kept_b, d_pred):
    norm_three, triple_weight, qv_bias, out_weight, out_bias, norm_four, head_weight, head_bias = (
        w_b
    )
    keep_three, x_three, triple, log_total, attn_mixed, a_four, keep_four, x_four = kept_b
    d_head_bias = jnp.sum(d_pred, axis=(0, 1))
    d_pred_low = d_pred.astype(jnp.bfloat16)
    d_head_w = jnp.einsum("npc,npd->cd", x_four, d_pred_low, preferred_element_type=jnp.float32)
    d_x_four = jnp.einsum(
        "npd,cd->npc", d_pred_low, head_weight, preferred_element_type=jnp.float32
    )
    d_h_two, d_norm_four = norm_backward(d_x_four * swish_grad(a_four), norm_four, keep_four)
    d_out_bias = jnp.sum(d_h_two, axis=(0, 1))
    d_proj_low = d_h_two.astype(jnp.bfloat16)
    d_out_w = jnp.einsum("npc,npd->cd", attn_mixed, d_proj_low, preferred_element_type=jnp.float32)
    d_mixed = jnp.einsum(
        "npd,cd->npc", d_proj_low, out_weight, preferred_element_type=jnp.float32
    ).astype(jnp.bfloat16)
    queries, attn_keys, attn_values = split_triple(triple)
    attn_probs = jnp.exp(attn_scores(queries, attn_keys) - log_total)
    d_values = jnp.einsum(
        "npq,npc->nqc", attn_probs.astype(jnp.bfloat16), d_mixed, preferred_element_type=jnp.float32
    )
    d_probs = jnp.einsum("npc,nqc->npq", d_mixed, attn_values, preferred_element_type=jnp.float32)
    d_scores = (
        attn_probs * (d_probs - jnp.sum(d_probs * attn_probs, axis=2, keepdims=True))
    ).astype(jnp.bfloat16)
    d_queries = jnp.einsum(
        "npq,nqc->npc", d_scores, attn_keys, preferred_element_type=jnp.float32
    ) * C ** (-0.5)
    d_keys = jnp.einsum(
        "npq,npc->nqc", d_scores, queries, preferred_element_type=jnp.float32
    ) * C ** (-0.5)
    d_triple = jnp.concatenate([d_queries, d_keys, d_values], axis=2).astype(jnp.bfloat16)
    d_triple_w = jnp.einsum("npc,npd->cd", x_three, d_triple, preferred_element_type=jnp.float32)
    d_triple_f = d_triple.astype(jnp.float32)
    d_qv_bias = jnp.concatenate(
        [jnp.sum(d_triple_f[..., :C], axis=(0, 1)), jnp.sum(d_triple_f[..., 2 * C :], axis=(0, 1))]
    )
    d_x_three = jnp.einsum(
        "npd,cd->npc", d_triple, triple_weight, preferred_element_type=jnp.float32
    )
    d_from_attn, d_norm_three = norm_backward(d_x_three, norm_three, keep_three)
    grads_b = [
        d_norm_three,
        d_triple_w,
        d_qv_bias,
        d_out_w,
        d_out_bias,
        d_norm_four,
        d_head_w,
        d_head_bias,
    ]
    return (d_h_two + d_from_attn, grads_b)


def adam_update(master, grad_in, first_mom, second, clip_scale):
    clipped = grad_in * clip_scale
    first_new = beta_one * first_mom + (1.0 - beta_one) * clipped
    second_new = beta_two * second + (1.0 - beta_two) * clipped * clipped
    first_hat = first_new / (1.0 - beta_one**STEP)
    second_hat = second_new / (1.0 - beta_two**STEP)
    master_new = master - learn_rate * (
        first_hat / (jnp.sqrt(second_hat) + adam_eps) + decay_rate * master
    )
    return (master_new, first_new, second_new)


def shard_reduce(vector):
    return lax.psum_scatter(vector, "fsdp", scatter_dimension=0, tiled=True)


def per_device(
    images,
    timesteps,
    labels,
    valid_slot,
    noise_idx,
    noise_table,
    params_a,
    params_b,
    first_a,
    second_a,
    first_b,
    second_b,
):
    w_a = unpack(fetch_weights(params_a), first_shapes())
    h_zero = images.astype(jnp.float32)
    h_one, kept_a = forward_first(w_a, h_zero, timesteps, labels)
    w_b = unpack(fetch_weights(params_b), second_shapes())
    predict, kept_b = forward_second(w_b, h_one)
    onehot_noise = (noise_idx[:, :, None] == jnp.arange(NT, dtype=jnp.int32)[None, None, :]).astype(
        jnp.float32
    )
    target = jnp.einsum(
        "npt,tc->npc",
        onehot_noise,
        noise_table,
        precision=highest,
        preferred_element_type=jnp.float32,
    )
    valid_f = valid_slot.astype(jnp.float32)
    differ = predict - target
    local_sum = jnp.sum(valid_f[:, None, None] * differ * differ)
    local_count = jnp.sum(valid_f) * POS
    loss_total, pixel_total = lax.psum((local_sum, local_count), ("dp", "fsdp"))
    d_pred = 2.0 / pixel_total * valid_f[:, None, None] * differ
    w_b_back = unpack(refetch_weights(params_b), second_shapes())
    d_h_one, grads_b = backward_second(w_b_back, kept_b, d_pred)
    flat_b = flatten(grads_b, PB)
    part_b = shard_reduce(flat_b)
    w_a_back = unpack(refetch_weights(params_a), first_shapes())
    grads_a = backward_first(w_a_back, kept_a, d_h_one)
    flat_a = flatten(grads_a, PA)
    part_a = shard_reduce(flat_a)
    part_a, part_b = lax.psum((part_a, part_b), "dp")
    squares = jnp.sum(part_a * part_a) + jnp.sum(part_b * part_b)
    norm_value = jnp.sqrt(lax.psum(squares, "fsdp"))
    clip_scale = jnp.minimum(1.0, clip_level / (norm_value + 1e-06))
    new_a, mom_one_a, mom_two_a = adam_update(params_a, part_a, first_a, second_a, clip_scale)
    new_b, mom_one_b, mom_two_b = adam_update(params_b, part_b, first_b, second_b, clip_scale)
    return (
        new_a,
        mom_one_a,
        mom_two_a,
        new_a.astype(jnp.bfloat16),
        new_b,
        mom_one_b,
        mom_two_b,
        new_b.astype(jnp.bfloat16),
        loss_total,
        pixel_total,
        norm_value,
    )


def solution(mesh):
    placed = (
        P(("dp", "fsdp"), None, None),
        P(("dp", "fsdp")),
        P(("dp", "fsdp")),
        P(("dp", "fsdp")),
        P(("dp", "fsdp"), None),
        P(),
        P("fsdp"),
        P("fsdp"),
        P("fsdp"),
        P("fsdp"),
        P("fsdp"),
        P("fsdp"),
    )
    return jax.shard_map(
        per_device,
        mesh=mesh,
        in_specs=placed,
        out_specs=(
            P("fsdp"),
            P("fsdp"),
            P("fsdp"),
            P("fsdp"),
            P("fsdp"),
            P("fsdp"),
            P("fsdp"),
            P("fsdp"),
            P(),
            P(),
            P(),
        ),
        check_vma=False,
    )
```

profile of v0, /device:TPU:0, one launch (start us, length us, event | category | flops | bytes accessed | tf_op | source)
XLA Modules:
  0.0 1031.6 jit_solution(10210352493190574518)
XLA Ops:
  11.4 42.5 %psum.35 = f32[]{:T(128)} all-reduce(f32[]{:T(128)S(6)} %mul.446), channel_id=1, replica_groups=mesh['dp'=2,'fsdp'=16] {'dp','fsdp'}, use_global_device_ids=true, to_apply=%region_19.20 | all-reduce | flops 1 | bytes 8 | tf_op jit(solution)/shard_map/psum | solution.py:419
  56.5 62.7 %all-gather.1 = bf16[16,1,20608]{2,1,0:T(2,128)(2,1)S(1)} all-gather(bf16[1,1,20608]{2,1,0:T(2,128)(2,1)S(1)} %reshape.1226), channel_id=1, replica_groups=mesh['dp'=2,'fsdp'=16] {'fsdp'}, dimensions={0}, use_global_device_ids=true | all-gather | bytes 700672 | tf_op jit(solution)/shard_map/all_gather | solution.py:69
  132.5 71.6 %reduce.70 = bf16[16,102912]{1,0:T(8,128)(2,1)} reduce(bf16[16,1,102912]{2,1,0:T(2,128)(2,1)} %all-gather.4.cloned.1.call-done, bf16[]{:T(256)} %constant.536), dimensions={1}, to_apply=%all-gather.reduce_sub_computation | reduce | bytes 6586370 | tf_op jit(solution)/shard_map/all_gather | solution.py:69
  204.1 7.6 reshape.1225
  340.1 7.9 fusion.42
  354.9 11.0 %scatter-add.61 = f32[8,18,18,256]{3,2,1,0:T(8,128)S(1)} dynamic-update-slice(f32[8,18,18,256]{3,2,1,0:T(8,128)S(1)} %scatter-add.60, f32[8,16,16,256]{3,2,1,0:T(8,128)} %fusion.36, s32[]{:T(128)} %constant.504.clone.1, s32[]{:T(128)} %bitcast.24, s32[]{:T(128)} %bitcast.25, s32[]{:T(128)} %constant.504.clone.1) | dynamic-update-slice | bytes 4194308 | tf_op jit(solution)/shard_map/scatter-add | solution.py:149
  371.3 11.1 %scatter-add.64 = f32[8,18,18,256]{3,2,1,0:T(8,128)S(1)} dynamic-update-slice(f32[8,18,18,256]{3,2,1,0:T(8,128)S(1)} %scatter-add.61, f32[8,16,16,256]{3,2,1,0:T(8,128)} %add_select_fusion.1, s32[]{:T(128)} %constant.504.clone.1, s32[]{:T(128)} %bitcast.27, s32[]{:T(128)} %bitcast.28, s32[]{:T(128)} %constant.504.clone.1) | dynamic-update-slice | bytes 4194308 | tf_op jit(solution)/shard_map/scatter-add | solution.py:149
  388.0 9.8 scatter-add.66
  401.2 9.8 scatter-add.69
  416.6 9.8 scatter-add.71
  429.8 9.8 scatter-add.74
  448.8 8.2 fusion.40
  504.1 11.0 %scatter-add.76 = f32[8,18,18,256]{3,2,1,0:T(8,128)S(1)} dynamic-update-slice(f32[8,18,18,256]{3,2,1,0:T(8,128)S(1)} %scatter-add.75, f32[8,16,16,256]{3,2,1,0:T(8,128)} %fusion.27, s32[]{:T(128)} %constant.504.clone.1, s32[]{:T(128)} %bitcast.24, s32[]{:T(128)} %bitcast.25, s32[]{:T(128)} %constant.504.clone.1) | dynamic-update-slice | bytes 4194308 | tf_op jit(solution)/shard_map/scatter-add | solution.py:149
  520.5 11.1 %scatter-add.79 = f32[8,18,18,256]{3,2,1,0:T(8,128)S(1)} dynamic-update-slice(f32[8,18,18,256]{3,2,1,0:T(8,128)S(1)} %scatter-add.76, f32[8,16,16,256]{3,2,1,0:T(8,128)} %add_select_fusion, s32[]{:T(128)} %constant.504.clone.1, s32[]{:T(128)} %bitcast.27, s32[]{:T(128)} %bitcast.28, s32[]{:T(128)} %constant.504.clone.1) | dynamic-update-slice | bytes 4194308 | tf_op jit(solution)/shard_map/scatter-add | solution.py:149
  537.1 9.8 scatter-add.81
  550.3 9.8 scatter-add.84
  565.6 9.8 scatter-add.86
  578.8 9.8 scatter-add.89
  596.1 20.3 %dynamic-update-slice.64 = f32[1646592]{0:T(1024)} dynamic-update-slice(f32[1646592]{0:T(1024)} %constant_dynamic-update-slice_fusion.36, f32[589824]{0:T(1024)S(1)} %bitcast.279, s32[]{} %constant.539) | dynamic-update-slice | bytes 4718596
  630.5 20.2 %dynamic-update-slice.74 = f32[1646592]{0:T(1024)} dynamic-update-slice(f32[1646592]{0:T(1024)} %constant_dynamic-update-slice_fusion.41, f32[589824]{0:T(1024)S(1)} %bitcast.278, s32[]{} %constant.558) | dynamic-update-slice | bytes 4718596
  668.2 242.8 %all-reduce.11.cloned.1.call-done = (f32[1646592]{0:T(1024)}, f32[329728]{0:T(1024)}) async-done(((f32[1646592]{0:T(1024)}, f32[329728]{0:T(1024)}), (f32[1646592]{0:T(1024)}, f32[329728]{0:T(1024)})) %all-reduce.11.cloned.1.call-update) | async-done | bytes 7905296
  914.5 17.9 %all-reduce.13.cloned.1.call-done = (f32[102912]{0:T(1024)}, f32[20608]{0:T(1024)}) async-done(((f32[102912]{0:T(1024)}, f32[20608]{0:T(1024)}), (f32[102912]{0:T(1024)}, f32[20608]{0:T(1024)})) %all-reduce.13.cloned.1.call-update) | async-done | bytes 494096 | tf_op jit(solution)/shard_map/psum | solution.py:429
  937.0 40.8 %psum.39 = f32[]{:T(128)} all-reduce(f32[]{:T(128)} %get-tuple-element.238), channel_id=1, replica_groups=mesh['dp'=2,'fsdp'=16] {'dp','fsdp'}, use_global_device_ids=true, to_apply=%region_59.60 | all-reduce | flops 1 | bytes 8 | tf_op jit(solution)/shard_map/psum | solution.py:419
  977.9 41.2 %psum.38 = f32[]{:T(128)} all-reduce(f32[]{:T(128)S(6)} %add.438), channel_id=1, replica_groups=mesh['dp'=2,'fsdp'=16] {'fsdp'}, use_global_device_ids=true, to_apply=%region_57.58 | all-reduce | flops 1 | bytes 8 | tf_op jit(solution)/shard_map/psum | solution.py:431
  (619 shorter events, 303.7 us)
Async XLA Ops:
  7.2 296.7 %copy-start = (f32[256,256]{1,0:T(8,128)S(1)}, f32[256,256]{1,0:T(8,128)}, u32[]{:S(2)}) copy-start(f32[256,256]{1,0:T(8,128)} %param.53) | copy-start | bytes 786436
  7.2 47.8 %copy-start.8 = (bf16[8,256,256]{2,1,0:T(8,128)(2,1)S(1)}, bf16[8,256,256]{2,1,0:T(8,128)(2,1)}, u32[]{:S(2)}) copy-start(bf16[8,256,256]{2,1,0:T(8,128)(2,1)} %param.48) | copy-start | bytes 3145732
  7.2 125.3 %all-gather.4.cloned.1.call-start = ((), (), s32[]{:S(2)}) async-start(), calls=%async_computation | async-start | bytes 6998016 | tf_op jit(solution)/shard_map/all_gather | solution.py:69
  8.4 48.0 %copy-start.163 = (s32[8]{0:T(128)S(1)}, s32[8]{0:T(128)}, u32[]{:S(2)}) copy-start(s32[8]{0:T(128)} %param.49) | copy-start | bytes 100
  8.4 48.0 %copy-start.82 = (f32[20608]{0:T(1024)S(1)}, f32[20608]{0:T(1024)}, u32[]{:S(2)}) copy-start(f32[20608]{0:T(1024)} %param.55) | copy-start | bytes 247300
  9.4 901.6 %all-reduce.11.cloned.1.call-start = ((), (), s32[]{:S(2)}) async-start(), calls=%async_computation.1 | async-start | bytes 15810560
  55.6 176.1 %copy-start.86 = (f32[8,256]{1,0:T(8,128)}, f32[8,256]{1,0:T(8,128)S(1)}, u32[]{:S(2)}) copy-start(f32[8,256]{1,0:T(8,128)S(1)} %sub.166) | copy-start | bytes 24580
  56.4 175.4 %copy-start.95 = (f32[8,256]{1,0:T(8,128)}, f32[8,256]{1,0:T(8,128)S(1)}, u32[]{:S(2)}) copy-start(f32[8,256]{1,0:T(8,128)S(1)} %mul.413) | copy-start | bytes 24580
  596.1 20.3 %copy-start.130 = (f32[256]{0:T(256)S(1)}, f32[256]{0:T(256)}, u32[]{:S(2)}) copy-start(f32[256]{0:T(256)} %get-tuple-element.244) | copy-start | bytes 3076
  596.1 23.5 %copy-start.132 = (f32[512]{0:T(512)S(1)}, f32[512]{0:T(512)}, u32[]{:S(2)}) copy-start(f32[512]{0:T(512)} %get-tuple-element.328) | copy-start | bytes 6148
  630.5 20.2 %copy-start.139 = (f32[256]{0:T(256)S(1)}, f32[256]{0:T(256)}, u32[]{:S(2)}) copy-start(f32[256]{0:T(256)} %get-tuple-element.261) | copy-start | bytes 3076
  630.5 22.8 %copy-start.136 = (f32[1,2,2,128]{3,1,2,0:T(2,128)S(1)}, f32[1,2,2,128]{3,1,2,0:T(2,128)}, u32[]{:S(2)}) copy-start(f32[1,2,2,128]{3,1,2,0:T(2,128)} %copy.141) | copy-start | bytes 6148
  630.5 24.1 %copy-start.65 = (f32[196608]{0:T(1024)S(1)}, f32[196608]{0:T(1024)}, u32[]{:S(2)}) copy-start(f32[196608]{0:T(1024)} %reshape.1220) | copy-start | bytes 2359300
  630.5 26.2 %copy-start.151 = (f32[256]{0:T(256)S(1)}, f32[256]{0:T(256)}, u32[]{:S(2)}) copy-start(f32[256]{0:T(256)} %get-tuple-element.228) | copy-start | bytes 3076
  630.5 27.5 %copy-start.150 = (f32[256]{0:T(256)S(1)}, f32[256]{0:T(256)}, u32[]{:S(2)}) copy-start(f32[256]{0:T(256)} %get-tuple-element.227) | copy-start | bytes 3076
  630.5 28.8 %copy-start.76 = (f32[32,2,8,128]{3,1,2,0:T(2,128)S(1)}, f32[32,2,8,128]{3,1,2,0:T(2,128)}, u32[]{:S(2)}) copy-start(f32[32,2,8,128]{3,1,2,0:T(2,128)} %copy.142) | copy-start | bytes 786436
  665.7 354.1 %copy-start.83 = (f32[20608]{0:T(1024)S(1)}, f32[20608]{0:T(1024)}, u32[]{:S(2)}) copy-start(f32[20608]{0:T(1024)} %param.55) | copy-start | bytes 247300
  665.7 354.1 %copy-start.101 = (f32[20608]{0:T(1024)S(1)}, f32[20608]{0:T(1024)}, u32[]{:S(2)}) copy-start(f32[20608]{0:T(1024)} %param.58) | copy-start | bytes 247300
  665.7 354.1 %copy-start.102 = (f32[20608]{0:T(1024)S(1)}, f32[20608]{0:T(1024)}, u32[]{:S(2)}) copy-start(f32[20608]{0:T(1024)} %param.59) | copy-start | bytes 247300
  665.7 355.7 %copy-start.70 = (f32[102912]{0:T(1024)S(1)}, f32[102912]{0:T(1024)}, u32[]{:S(2)}) copy-start(f32[102912]{0:T(1024)} %param.54) | copy-start | bytes 1234948
  665.7 355.7 %copy-start.79 = (f32[102912]{0:T(1024)S(1)}, f32[102912]{0:T(1024)}, u32[]{:S(2)}) copy-start(f32[102912]{0:T(1024)} %param.56) | copy-start | bytes 1234948
  665.7 355.7 %copy-start.80 = (f32[102912]{0:T(1024)S(1)}, f32[102912]{0:T(1024)}, u32[]{:S(2)}) copy-start(f32[102912]{0:T(1024)} %param.57) | copy-start | bytes 1234948
  665.7 266.7 %all-reduce.13.cloned.1.call-start = ((), (), s32[]{:S(2)}) async-start(), calls=%async_computation.2 | async-start | bytes 999424 | tf_op jit(solution)/shard_map/psum | solution.py:429
  932.5 91.3 %copy-start.1 = (f32[256,256]{1,0:T(8,128)S(1)}, f32[256,256]{1,0:T(8,128)}, u32[]{:S(2)}) copy-start(f32[256,256]{1,0:T(8,128)} %param.53) | copy-start | bytes 786436
  (150 other events, 487.3 us)
Sparse Core Ops, SparseCore 0:
  11.3 117.6 all-gather.3
  665.8 245.1 all-reduce.10
  914.7 17.7 all-reduce.12
where the time goes:
time: 1050 us; the launch traced here: 1030 us
  local copies, waits for them, and re-layouts  311 us (30%)
  waiting for transfers between devices  261 us (25%)
  blocking collectives  187 us (18%)
  other arithmetic  185 us (18%)
  matrix products  65.3 us (6%)
  between operations  22 us (2%)
    unnamed x4, waiting for transfers between devices  243 us
    unnamed x411, local copies, waits for them, and re-layouts  136 us
    scatter-add x14, local copies, waits for them, and re-layouts, conv_backward(): d_padded.at[:, r:r + SIDE, s:s + SIDE, :].add(d_cols[:, :, :, r * 3 + s, :])  123 us
    psum x2, blocking collectives, per_device(): loss_total, pixel_total = lax.psum((local_sum, local_count), ('dp', 'fsdp'))  83.3 us
    all_gather x2, other arithmetic, fetch_weights(): lax.all_gather(vector.astype(jnp.bfloat16), 'fsdp', axis=0, tiled=True)  75.6 us
    all_gather x1, blocking collectives, fetch_weights(): lax.all_gather(vector.astype(jnp.bfloat16), 'fsdp', axis=0, tiled=True)  62.7 us
    psum x1, blocking collectives, per_device(): norm_value = jnp.sqrt(lax.psum(squares, 'fsdp'))  41.2 us
    add x10, other arithmetic, conv_backward(): d_padded.at[:, r:r + SIDE, s:s + SIDE, :].add(d_cols[:, :, :, r * 3 + s, :])  37.2 us
  transfers between devices with their start and end apart: 3, of which 2 were waited for; matrix products, arithmetic and copies ran while one was open for 2% of the time, Pallas kernels for 0%

commit v1 on v0

v1 whole, which is shorter than its diff:
```python
import functools
import math
import jax
import jax.numpy as jnp
import numpy as np
from jax import lax
from jax.experimental import pallas as pl
from jax.experimental.pallas import tpu as pltpu
from jax.sharding import PartitionSpec as P

C = 256
SIDE = 16
POS = 256
TE = 512
SIN = 128
NCLS = 10
NT = 256
NIMG = 8
bf = jnp.bfloat16
f32 = jnp.float32
eps_norm = 1e-05
CH = 64
TY = 2

A_N1, A_K1, A_B1, A_W1, A_TB1, A_W2, A_TB2, A_CT, A_PT, A_PB, A_N2, A_K2, A_B2 = (
    0, 2, 2306, 2307, 2563, 2565, 3589, 3591, 3611, 4123, 4124, 4126, 6430)
A_ROWS = 6432
B_N3, B_W, B_QV, B_WO, B_BO, B_N4, B_WH, B_BH = (0, 2, 770, 772, 1028, 1029, 1031, 1287)
B_ROWS = 1288


def dot(a, b):
    return jnp.dot(a, b, preferred_element_type=f32)


def dot_nt(a, b):
    return lax.dot_general(a, b, (((1,), (1,)), ((), ())), preferred_element_type=f32)


def dot_tn(a, b):
    return lax.dot_general(a, b, (((0,), (0,)), ((), ())), preferred_element_type=f32)


def split3(x):
    hi = x.astype(bf).astype(f32)
    rest = x - hi
    mid = rest.astype(bf).astype(f32)
    return hi, mid, rest - mid


def wide_dot(x, w, nt=False):
    n = x.shape[0]
    stacked = jnp.concatenate(split3(x), axis=0).astype(bf)
    out = dot_nt(stacked, w) if nt else dot(stacked, w)
    return out[:n] + out[n:2 * n] + out[2 * n:]


def outer_sum(a, b):
    a0, a1, _ = split3(a)
    b0, b1, _ = split3(b)
    return dot_tn(jnp.concatenate([a0, a0, a1], axis=0).astype(bf),
                  jnp.concatenate([b0, b1, b0], axis=0).astype(bf))


def sigm(v):
    return 0.5 * jnp.tanh(0.5 * v) + 0.5


def rowsum(x):
    return jnp.sum(x, axis=0, keepdims=True)


def put_shifts(buf, i, r0, x):
    n = x.shape[0]
    col = lax.broadcasted_iota(jnp.int32, x.shape, 0) & 15
    left = jnp.where(col == 0, 0.0, pltpu.roll(x, 1, 0))
    right = jnp.where(col == 15, 0.0, pltpu.roll(x, n - 1, 0))
    y = n // 16
    for s, v in enumerate((left, x, right)):
        buf[pl.ds(1 + r0 // 16, y), i, :, 256 * s:256 * s + 256] = v.astype(bf).reshape(y, 16, C)


def conv_mm(buf, kmat, y, ty=TY):
    parts = [buf[pl.ds(y + r, ty)].reshape(ty * 128, 3 * C) for r in range(3)]
    return dot(jnp.concatenate(parts, axis=1), kmat[...])


class Refs:
    pass


def ld(f, row, n, stride=1):
    at = pl.ds(row, n, stride=stride) if stride > 1 else pl.ds(row, n)
    return jnp.concatenate([f[0, at, :], f[1, at, :]], axis=1)


def st(f, row, value, stride=1):
    n = value.shape[0]
    at = pl.ds(row, n, stride=stride) if stride > 1 else pl.ds(row, n)
    f[0, at, :] = value[:, :128]
    f[1, at, :] = value[:, 128:]


def unpack_weights(R, fa, fb):
    for kmat, kt, base in ((R.k1, R.k1t, A_K1), (R.k2, R.k2t, A_K2)):
        for t in range(9):
            w = ld(fa, base + 256 * t, 256)
            kmat[256 * t:256 * t + 256, :] = w.astype(bf)
            kt[256 * (8 - t):256 * (8 - t) + 256, :] = w.T.astype(bf)
    for h in range(2):
        R.tw1[:, 256 * h:256 * h + 256] = ld(fa, A_W1 + h, SIN, 2).astype(bf)
        R.tw2[:, 256 * h:256 * h + 256] = ld(fa, A_W2 + h, TE, 2).astype(bf)
    R.pt[...] = ld(fa, A_PT, TE).astype(bf)
    for h in range(3):
        w = ld(fb, B_W + h, C, 3)
        R.wt[:, 256 * h:256 * h + 256] = w.astype(bf)
        R.wtt[256 * h:256 * h + 256, :] = w.T.astype(bf)
    w = ld(fb, B_WO, C)
    R.wo[...] = w.astype(bf)
    R.wot[...] = w.T.astype(bf)
    w = ld(fb, B_WH, C)
    R.wh[...] = w.astype(bf)
    R.wht[...] = w.T.astype(bf)
    for k, row in enumerate((A_N1, A_N1 + 1, A_B1, A_TB1, A_TB1 + 1, A_TB2, A_TB2 + 1, A_PB, A_N2, A_N2 + 1, A_B2)):
        R.vec[k:k + 1, :] = ld(fa, row, 1)
    for k, row in enumerate((B_N3, B_N3 + 1, B_QV, B_QV + 1, B_BO, B_N4, B_N4 + 1, B_BH)):
        R.vec[11 + k:12 + k, :] = ld(fb, row, 1)
    R.ct[0:20, :] = ld(fa, A_CT, 20)


(V_G1, V_C1, V_B1, V_TB1, V_TB1B, V_TB2, V_TB2B, V_PB, V_G2, V_C2, V_B2,
 V_G3, V_C3, V_QB, V_VB, V_BO, V_G4, V_C4, V_BH) = range(19)


def vec(R, k):
    return R.vec[k:k + 1, :]


def group_mean(R, s):
    return wide_dot(s, R.gm[...])


def stats(R, k, load):
    for i in range(NIMG):
        R.tmp[i:i + 1, :] = rowsum(load(i))
    mean = group_mean(R, R.tmp[0:8, :])
    R.mean[k] = mean
    for i in range(NIMG):
        x = load(i) - mean[i:i + 1, :]
        R.tmp[i:i + 1, :] = rowsum(x * x)
    R.inv[k] = lax.rsqrt(group_mean(R, R.tmp[0:8, :]) + eps_norm)


def norm_sums(R, k, gain):
    s1, s2 = R.s1[...], R.s2[...]
    m = group_mean(R, jnp.concatenate([s1 * gain, s2 * gain], axis=0))
    R.m1[...] = m[:8] * R.inv[k]
    R.m2[...] = m[8:] * R.inv[k]
    return rowsum(s2), rowsum(s1)


def first_setup(R):
    row = lax.broadcasted_iota(jnp.int32, (C, C), 0) >> 3
    col = lax.broadcasted_iota(jnp.int32, (C, C), 1) >> 3
    R.gm[...] = jnp.where(row == col, 1.0 / 2048.0, 0.0).astype(bf)
    zero = jnp.zeros((1, NIMG, 16, 3 * C), bf)
    for buf in (R.buf1, R.buf2, R.dbuf):
        buf[0:1] = zero
        buf[17:18] = zero
    hi, mid, lo = split3(R.table[...])
    R.tab3[...] = jnp.concatenate([hi, mid, lo], axis=1).astype(bf)

    @pl.loop(0, NIMG)
    def _(i):
        rows = lax.broadcasted_iota(jnp.int32, (NT, POS), 0)
        hot = jnp.where(rows == R.nidx[pl.ds(i, 1), :], 1.0, 0.0)
        out = dot(hot.T.astype(bf), R.tab3[...])
        R.target[i] = out[:, :C] + out[:, C:2 * C] + out[:, 2 * C:]
    stats(R, 0, lambda i: R.img[i].astype(f32))


def column_of(smem, shape):
    row = lax.broadcasted_iota(jnp.int32, shape, 0)
    out = jnp.zeros(shape, jnp.int32)
    for i in range(NIMG):
        out = jnp.where(row == i, smem[i], out)
    return out


def time_forward(R):
    lane = lax.broadcasted_iota(jnp.int32, (NIMG, SIN), 1)
    factor = math.log(10000.0) / (SIN // 2 - 1)
    freq = jnp.exp((lane & 63).astype(f32) * -factor)
    angle = column_of(R.steps, (NIMG, SIN)).astype(f32) * freq
    e = jnp.where(lane < 64, jnp.sin(angle), jnp.cos(angle))
    R.emb[...] = e
    u = wide_dot(e, R.tw1[...]) + jnp.concatenate([vec(R, V_TB1), vec(R, V_TB1B)], axis=1)
    R.pre[...] = u
    lab = column_of(R.labels, (NIMG, TE))
    te = wide_dot(u * sigm(u), R.tw2[...]) + jnp.concatenate([vec(R, V_TB2), vec(R, V_TB2B)], axis=1)
    for j in range(NCLS):
        row = jnp.concatenate([R.ct[2 * j:2 * j + 1, :], R.ct[2 * j + 1:2 * j + 2, :]], axis=1)
        te = te + jnp.where(lab == j, row, 0.0)
    R.te[...] = te
    add = wide_dot(te * sigm(te), R.pt[...]) + vec(R, V_PB) + vec(R, V_B1)
    for i in range(NIMG):
        R.addb[i] = jnp.broadcast_to(add[i:i + 1, :], (16, C))


def each_chunk(fn):
    @pl.loop(0, NIMG)
    def _(i):
        for c in range(POS // CH):
            fn(i, c * CH)


def normed(R, k, i, x):
    return (x - R.mean[k, pl.ds(i, 1), :]) * R.inv[k, pl.ds(i, 1), :]


def forward_a(R):
    def one(i, r0):
        x = normed(R, 0, i, R.img[i, r0:r0 + CH, :].astype(f32))
        a = x * vec(R, V_G1) + vec(R, V_C1)
        put_shifts(R.buf1, i, r0, a * sigm(a))
    each_chunk(one)

    @pl.loop(0, SIDE // TY)
    def _(t):
        acc = conv_mm(R.buf1, R.k1, t * TY).reshape(TY, NIMG, 16, C)
        for yy in range(TY):
            R.c1[:, pl.ds(pl.multiple_of((t * TY + yy) * 16, 16), 16), :] = acc[yy] + R.addb[...]
    stats(R, 1, lambda i: R.c1[i])

    def two(i, r0):
        x = normed(R, 1, i, R.c1[i, r0:r0 + CH, :])
        a = x * vec(R, V_G2) + vec(R, V_C2)
        put_shifts(R.buf2, i, r0, a * sigm(a))
    each_chunk(two)

    @pl.loop(0, SIDE // TY)
    def _(t):
        acc = conv_mm(R.buf2, R.k2, t * TY).reshape(TY, NIMG, 16, C)
        for yy in range(TY):
            at = pl.ds(pl.multiple_of((t * TY + yy) * 16, 16), 16)
            R.h1[:, at, :] = acc[yy] + R.img[:, at, :].astype(f32) + vec(R, V_B2)
    stats(R, 2, lambda i: R.h1[i])


def forward_b(R):
    bias = jnp.concatenate([vec(R, V_QB), jnp.zeros((1, C), f32), vec(R, V_VB)], axis=1)

    @pl.loop(0, NIMG)
    def _(i):
        x = (normed(R, 2, i, R.h1[i]) * vec(R, V_G3) + vec(R, V_C3)).astype(bf)
        R.x3t[:, pl.ds(pl.multiple_of(i * POS, POS), POS)] = x.T
        R.tri[i] = (dot(x, R.wt[...]) + bias).astype(bf)

    @pl.loop(0, NIMG)
    def _(i):
        k = R.tri[i, :, C:2 * C]
        v = R.tri[i, :, 2 * C:]
        for h in range(2):
            at = slice(128 * h, 128 * h + 128)
            s = dot_nt(R.tri[i, at, 0:C], k) * C ** (-0.5)
            e = jnp.exp(s - jnp.max(s, axis=1, keepdims=True))
            p = e * (1.0 / jnp.sum(e, axis=1, keepdims=True))
            R.p[i, at, :] = p
            o = dot(p.astype(bf), v).astype(bf)
            R.o[i, at, :] = o
            R.h2[i, at, :] = R.h1[i, at, :] + dot(o, R.wo[...]) + vec(R, V_BO)
    stats(R, 3, lambda i: R.h2[i])


def head(R, scale):
    R.loss[...] = jnp.zeros_like(R.loss)
    R.sh[...] = jnp.zeros_like(R.sh)

    @pl.loop(0, NIMG)
    def _(i):
        valid = R.valid[i].astype(f32)
        s1 = jnp.zeros((1, C), f32)
        s2 = jnp.zeros((1, C), f32)
        for h in range(2):
            at = slice(128 * h, 128 * h + 128)
            x = normed(R, 3, i, R.h2[i, at, :])
            a = x * vec(R, V_G4) + vec(R, V_C4)
            sg = sigm(a)
            x4 = (a * sg).astype(bf)
            R.xt[:, pl.ds(pl.multiple_of(i * POS + 128 * h, 128), 128)] = x4.T
            differ = dot(x4, R.wh[...]) + vec(R, V_BH) - R.target[i, at, :]
            dv = valid * differ
            R.loss[...] += rowsum(dv * differ)
            dp = dv * scale
            R.sh[...] += rowsum(dp)
            low = dp.astype(bf)
            R.low[i, at, :] = low
            da = dot(low, R.wht[...]) * (sg * (1.0 + a * (1.0 - sg)))
            R.da[i, at, :] = da
            s1 += rowsum(da)
            s2 += rowsum(da * x)
        R.s1[pl.ds(i, 1), :] = s1
        R.s2[pl.ds(i, 1), :] = s2


def weight_grad(R, xt, low, put):
    put(dot(xt[...], low[...].reshape(NIMG * POS, low.shape[-1])))


def backward_b(R):
    st(R.gb, B_BH, R.sh[...])
    st(R.gb, B_WH, dot(R.xt[...], R.low[...].reshape(NIMG * POS, C)))
    dg, db = norm_sums(R, 3, vec(R, V_G4))
    st(R.gb, B_N4, dg)
    st(R.gb, B_N4 + 1, db)
    R.sh[...] = jnp.zeros_like(R.sh)
    R.sq[...] = jnp.zeros_like(R.sq)

    @pl.loop(0, NIMG)
    def _(i):
        x = normed(R, 3, i, R.h2[i])
        d = (R.inv[3, pl.ds(i, 1), :] * vec(R, V_G4)) * R.da[i] - R.m1[pl.ds(i, 1), :] - x * R.m2[pl.ds(i, 1), :]
        R.dh[i] = d
        R.sh[...] += rowsum(d)
        low = d.astype(bf)
        R.low[i] = low
        R.xt[:, pl.ds(pl.multiple_of(i * POS, POS), POS)] = R.o[i].T
        dm = dot(low, R.wot[...]).astype(bf)
        p = R.p[i]
        q = R.tri[i, :, 0:C]
        k = R.tri[i, :, C:2 * C]
        v = R.tri[i, :, 2 * C:]
        dv = dot_tn(p.astype(bf), dm).astype(bf)
        dpr = dot_nt(dm, v)
        ds = (p * (dpr - jnp.sum(dpr * p, axis=1, keepdims=True))).astype(bf)
        dq = (dot(ds, k) * C ** (-0.5)).astype(bf)
        dk = (dot_tn(ds, q) * C ** (-0.5)).astype(bf)
        R.tri[i, :, 0:C] = dq
        R.tri[i, :, C:2 * C] = dk
        R.tri[i, :, 2 * C:] = dv
        R.sq[:, 0:C] += rowsum(dq.astype(f32))
        R.sq[:, C:2 * C] += rowsum(dv.astype(f32))
    st(R.gb, B_BO, R.sh[...])
    st(R.gb, B_QV, R.sq[:, 0:C])
    st(R.gb, B_QV + 1, R.sq[:, C:2 * C])
    st(R.gb, B_WO, dot(R.xt[...], R.low[...].reshape(NIMG * POS, C)))

    @pl.loop(0, NIMG)
    def _(i):
        da = dot(R.tri[i], R.wtt[...])
        R.da[i] = da
        R.s1[pl.ds(i, 1), :] = rowsum(da)
        R.s2[pl.ds(i, 1), :] = rowsum(da * normed(R, 2, i, R.h1[i]))
    for h in range(3):
        st(R.gb, B_W + h, dot(
            R.x3t[...], R.tri[:, :, 256 * h:256 * h + 256].reshape(NIMG * POS, C)), 3)
    dg, db = norm_sums(R, 2, vec(R, V_G3))
    st(R.gb, B_N3, dg)
    st(R.gb, B_N3 + 1, db)


def kernel_grad(R, buf, row):
    @pl.loop(0, SIDE // 2)
    def _(t):
        x = buf[pl.ds(1 + 2 * t, 2), :, :, C:2 * C].reshape(256, C)
        R.xt[:, pl.ds(pl.multiple_of(t * 256, 256), 256)] = x.T
    for r in range(3):
        for s in range(3):
            d = R.dbuf[2 - r:18 - r, :, :, 256 * (2 - s):256 * (3 - s)].reshape(NIMG * POS, C)
            at = row + (3 * r + s) * 256
            st(R.ga, at, dot(R.xt[...], d))


def conv_back(R, kt):
    @pl.loop(0, SIDE // TY)
    def _(t):
        acc = conv_mm(R.dbuf, kt, t * TY).reshape(TY, NIMG, 16, C)
        for yy in range(TY):
            R.da[:, pl.ds(pl.multiple_of((t * TY + yy) * 16, 16), 16), :] = acc[yy]


def swish_back(R, k, load, vg, vc, keep):
    R.s1[...] = jnp.zeros_like(R.s1)
    R.s2[...] = jnp.zeros_like(R.s2)

    def one(i, r0):
        x = normed(R, k, i, load(i, r0))
        a = x * vec(R, vg) + vec(R, vc)
        sg = sigm(a)
        da = R.da[i, r0:r0 + CH, :] * (sg * (1.0 + a * (1.0 - sg)))
        if keep:
            R.da[i, r0:r0 + CH, :] = da
        R.s1[pl.ds(i, 1), :] += rowsum(da)
        R.s2[pl.ds(i, 1), :] += rowsum(da * x)
    each_chunk(one)


def backward_a(R):
    R.sh[...] = jnp.zeros_like(R.sh)

    def one(i, r0):
        at = slice(r0, r0 + CH)
        x = normed(R, 2, i, R.h1[i, at, :])
        d = (R.dh[i, at, :] + (R.inv[2, pl.ds(i, 1), :] * vec(R, V_G3)) * R.da[i, at, :]
             - R.m1[pl.ds(i, 1), :] - x * R.m2[pl.ds(i, 1), :])
        R.sh[...] += rowsum(d)
        put_shifts(R.dbuf, i, r0, d)
    each_chunk(one)
    st(R.ga, A_B2, R.sh[...])
    kernel_grad(R, R.buf2, A_K2)
    conv_back(R, R.k2t)
    swish_back(R, 1, lambda i, r0: R.c1[i, r0:r0 + CH, :], V_G2, V_C2, True)
    dg, db = norm_sums(R, 1, vec(R, V_G2))
    st(R.ga, A_N2, dg)
    st(R.ga, A_N2 + 1, db)
    R.tmp[...] = jnp.zeros_like(R.tmp)

    def two(i, r0):
        at = slice(r0, r0 + CH)
        x = normed(R, 1, i, R.c1[i, at, :])
        d = ((R.inv[1, pl.ds(i, 1), :] * vec(R, V_G2)) * R.da[i, at, :]
             - R.m1[pl.ds(i, 1), :] - x * R.m2[pl.ds(i, 1), :])
        R.tmp[pl.ds(i, 1), :] += rowsum(d)
        put_shifts(R.dbuf, i, r0, d)
    each_chunk(two)
    time_backward(R)
    kernel_grad(R, R.buf1, A_K1)
    conv_back(R, R.k1t)
    swish_back(R, 0, lambda i, r0: R.img[i, r0:r0 + CH, :].astype(f32), V_G1, V_C1, False)
    st(R.ga, A_N1, rowsum(R.s2[...]))
    st(R.ga, A_N1 + 1, rowsum(R.s1[...]))


def swish_slope(v):
    s = sigm(v)
    return s * (1.0 + v * (1.0 - s))


def time_backward(R):
    d_add = R.tmp[0:8, :]
    total = rowsum(d_add)
    st(R.ga, A_B1, total)
    st(R.ga, A_PB, total)
    te = R.te[...]
    st(R.ga, A_PT, outer_sum(te * sigm(te), d_add))
    d_te = wide_dot(d_add, R.pt[...], nt=True) * swish_slope(te)
    lab = column_of(R.labels, (NIMG, TE))
    for j in range(NCLS):
        row = rowsum(jnp.where(lab == j, d_te, 0.0))
        for h in range(2):
            st(R.ga, A_CT + 2 * j + h, row[:, 256 * h:256 * h + 256])
    row = rowsum(d_te)
    u = R.pre[...]
    dw2 = outer_sum(u * sigm(u), d_te)
    d_u = wide_dot(d_te, R.tw2[...], nt=True) * swish_slope(u)
    row1 = rowsum(d_u)
    dw1 = outer_sum(R.emb[...], d_u)
    for h in range(2):
        st(R.ga, A_TB2 + h, row[:, 256 * h:256 * h + 256])
        st(R.ga, A_TB1 + h, row1[:, 256 * h:256 * h + 256])
        st(R.ga, A_W2 + h, dw2[:, 256 * h:256 * h + 256], 2)
        st(R.ga, A_W1 + h, dw1[:, 256 * h:256 * h + 256], 2)


SCRATCH = dict(
    k1=((2304, C), bf), k1t=((2304, C), bf), k2=((2304, C), bf), k2t=((2304, C), bf),
    tw1=((SIN, TE), bf), tw2=((TE, TE), bf), pt=((TE, C), bf),
    wt=((C, 3 * C), bf), wtt=((3 * C, C), bf), wo=((C, C), bf), wot=((C, C), bf), wh=((C, C), bf), wht=((C, C), bf),
    vec=((24, C), f32), ct=((24, C), f32),
    gm=((C, C), bf), tab3=((NT, 3 * C), bf), target=((NIMG, POS, C), f32),
    tmp=((8, C), f32), mean=((4, 8, C), f32), inv=((4, 8, C), f32),
    s1=((8, C), f32), s2=((8, C), f32), m1=((8, C), f32), m2=((8, C), f32),
    sh=((1, C), f32), sq=((1, 2 * C), f32),
    emb=((8, SIN), f32), pre=((8, TE), f32), te=((8, TE), f32), addb=((8, 16, C), f32),
    buf1=((18, 8, 16, 3 * C), bf), buf2=((18, 8, 16, 3 * C), bf), dbuf=((18, 8, 16, 3 * C), bf),
    c1=((8, POS, C), f32), h1=((8, POS, C), f32), h2=((8, POS, C), f32), da=((8, POS, C), f32), dh=((8, POS, C), f32),
    p=((8, POS, POS), f32), o=((8, POS, C), bf), low=((8, POS, C), bf),
    tri=((8, POS, 3 * C), bf),
    x3t=((C, 8 * POS), bf), xt=((C, 8 * POS), bf),
)


def main_kernel(names_in, *refs):
    R = Refs()
    n_in = len(names_in)
    for name, r in zip(names_in, refs):
        setattr(R, name, r)
    R.ga, R.gb, R.loss = refs[n_in:n_in + 3]
    for name, r in zip(list(SCRATCH), refs[n_in + 3:]):
        setattr(R, name, r)
    fa, fb = R.ga, R.gb
    for c in range(0, A_ROWS, 402):
        st(fa, c, R.wa[c:c + 402, :].astype(f32))
    st(fb, 0, R.wb[...].astype(f32))
    first_setup(R)
    unpack_weights(R, fa, fb)
    time_forward(R)
    forward_a(R)
    forward_b(R)
    head(R, R.scale[0])
    backward_b(R)
    backward_a(R)


def compute(img, steps, labels, valid, scale, nidx, table, wa, wb):
    smem = pl.BlockSpec(memory_space=pltpu.SMEM)
    vmem = pl.BlockSpec(memory_space=pltpu.VMEM)
    names = ("img", "steps", "labels", "valid", "scale", "nidx", "table", "wa", "wb")
    return pl.pallas_call(
        functools.partial(main_kernel, names),
        out_shape=(jax.ShapeDtypeStruct((2, A_ROWS, 128), f32), jax.ShapeDtypeStruct((2, B_ROWS, 128), f32),
                   jax.ShapeDtypeStruct((1, C), f32)),
        in_specs=[vmem, smem, smem, smem, smem, vmem, vmem, vmem, vmem],
        out_specs=(vmem, vmem, vmem),
        scratch_shapes=[pltpu.VMEM(s, d) for s, d in SCRATCH.values()],
        compiler_params=pltpu.CompilerParams(vmem_limit_bytes=63 * 1024 * 1024),
    )(img, steps, labels, valid, scale, nidx, table, wa, wb)


beta_one = 0.5
beta_two = 0.5
learn_rate = 0.1
decay_rate = 0.01
adam_eps = 1e-08
clip_level = 0.01
STEP = 5
PA = A_ROWS * C
PB = B_ROWS * C
MESH = pl.DeviceIdType.MESH
ORDER = (0, 1, 3, 2)
HALF_A, HALF_B, PIECE = 201, 48, 256
B_AT = 208


class Place:
    def __init__(self, chips):
        self.me = lax.axis_index("fsdp")
        self.core = lax.axis_index("dp")
        self.depth = chips // 4

    def z(self, k, d):
        return lax.rem(lax.div(k, 4) + d + self.depth, self.depth) * 4 + lax.rem(k, 4)

    def flip_x(self, k):
        return k + 1 - 2 * lax.rem(k, 2)

    def flip_y(self, k):
        return k + 2 - 4 * lax.rem(lax.div(k, 2), 2)

    def s(self, k):
        return self.core * self.flip_x(k) + (1 - self.core) * self.flip_y(k)

    def t(self, k):
        return self.core * self.flip_y(k) + (1 - self.core) * self.flip_x(k)

    def pieces(self):
        line = [self.z(self.me, -j) for j in range(4)]
        near = line + [self.s(k) for k in line]
        return near + [self.t(k) for k in near]


def send(src, dst, sems, at, core, chip):
    copy = pltpu.make_async_remote_copy(
        src_ref=src, dst_ref=dst, send_sem=sems[0].at[at], recv_sem=sems[1].at[at],
        device_id=(core, chip), device_id_type=MESH)
    copy.start()
    return copy


def greet(R, place, chips):
    barrier = pltpu.get_barrier_semaphore()
    for d in range(1, chips):
        pl.semaphore_signal(barrier, inc=1, device_id=(place.core, lax.rem(place.me + d, chips)), device_id_type=MESH)
    pl.semaphore_signal(barrier, inc=1, device_id=(1 - place.core, place.me), device_id_type=MESH)
    return barrier


def own_piece(R, place):
    count = R.valid[0]
    for i in range(1, NIMG):
        count = count + R.valid[i]
    count = count.astype(f32)
    odd = lax.rem(place.me, 2) == 1
    R.flat[0:8, :] = jnp.zeros((8, 128), f32)
    R.flat[168:184, :] = jnp.zeros((16, 128), f32)
    R.flat[8:169, :] = R.pb[...]
    for h in range(2):
        for lane in range(2):
            R.piece[lane, 0:201, :] = R.pa[pl.ds(402 * h + lane, 201, stride=2), :]
            even_rows = R.flat[pl.ds(8 + lane + 96 * h, 48 - 8 * h, stride=2), :]
            odd_rows = R.flat[pl.ds(7 + lane + 96 * h, 48 - 8 * h, stride=2), :]
            R.piece[lane, 208:256 - 8 * h, :] = jnp.where(odd, odd_rows, even_rows)
        R.piece[:, 201:208, :] = jnp.full((2, 7, 128), count)

        @pl.when(place.core == h)
        def _():
            R.w[place.me, h] = jnp.concatenate([R.piece[0], R.piece[1]], axis=1).astype(bf)


def gather_weights(R, place):
    me, core = place.me, place.core
    got = place.pieces()
    put = lambda k: R.w.at[k, core]
    over_s, over_t = place.s(me), place.t(me)
    zc = {d: send(put(me), put(me), R.zsem, d - 1, core, place.z(me, d)) for d in (1, 3, 2)}
    sc, tc, sib = {}, {}, {}
    for j in ORDER:
        if j:
            zc[j].wait_recv()
        sc[j] = send(put(got[j]), put(got[j]), R.ssem, j, core, over_s)
        tc[j] = send(put(got[j]), put(got[j]), R.tsem, j, core, over_t)
        sib[j] = send(put(got[j]), put(got[j]), R.csem, j, 1 - core, me)
    for j in ORDER:
        sc[j].wait_recv()
        q = 4 + j
        tc[q] = send(put(got[q]), put(got[q]), R.tsem, q, core, over_t)
        sib[q] = send(put(got[q]), put(got[q]), R.csem, q, 1 - core, me)
    for half in (0, 4):
        for j in ORDER:
            q = half + j
            tc[q].wait_recv()
            sib[8 + q] = send(put(got[8 + q]), put(got[8 + q]), R.csem, 8 + q, 1 - core, me)
    for c in sib.values():
        c.wait_recv()
    for group in (zc, sc, tc, sib):
        for c in group.values():
            c.wait_send()


def spread_rows(R, chips):
    count = jnp.zeros((1, 128), f32)
    for k in range(chips):
        base = (161 * k) // 2
        odd = k % 2
        for h in range(2):
            a = R.w[k, h, 0:208, :].astype(f32)
            row = 402 * k + 201 * h
            R.ga[0, row:row + 208, :] = a[:, :128]
            R.ga[1, row:row + 208, :] = a[:, 128:]
            count = count + a[201:202, :128]
            b = R.w[k, h, 208:256, :].astype(f32)
            if h == 0:
                R.gb[0, base + odd:base + 48, :] = b[odd:, :128]
                R.gb[1, base:base + 48, :] = b[:, 128:]
            else:
                R.gb[0, base + 48:base + 81, :] = b[:33, :128]
                R.gb[1, base + 48:base + 80 + odd, :] = b[:32 + odd, 128:]
    return count


def pack_gradients(R, chips):
    for k in range(chips):
        base = (161 * k) // 2
        for h in range(2):
            R.w[k, h, 0:208, :] = ld(R.ga, 402 * k + 201 * h, 208).astype(bf)
            R.w[k, h, 208:256, :] = ld(R.gb, base + 48 * h, 48).astype(bf)


def reduce_gradients(R, place):
    me, core = place.me, place.core
    got = place.pieces()
    over_s, over_t = place.s(me), place.t(me)
    order = [12 + j for j in ORDER] + [8 + j for j in ORDER]
    sib = {}
    for q in order[:4] + [4 + j for j in ORDER] + order[4:] + [1, 3, 2, 0]:
        there = q + 4 if 4 <= q < 8 else q - 4 if 8 <= q < 12 else q
        copy = pltpu.make_async_remote_copy(
            src_ref=R.w.at[got[q], 1 - core], dst_ref=R.r1.at[there], send_sem=R.gcsem[0].at[q],
            recv_sem=R.gcsem[1].at[there], device_id=(1 - core, me), device_id_type=MESH)
        copy.start()
        sib[there] = copy

    def total(q):
        return R.w[got[q], core].astype(f32) + R.r1[q].astype(f32)
    tc, sc, zc = {}, {}, {}
    for q in order:
        sib[q].wait_recv()
        R.t2[q - 8] = total(q).astype(bf)
        tc[q - 8] = send(R.t2.at[q - 8], R.r2.at[q - 8], R.gtsem, q - 8, core, over_t)
    for j in ORDER:
        q = 4 + j
        sib[q].wait_recv()
        tc[q].wait_recv()
        R.t3[j] = (total(q) + R.r2[q].astype(f32)).astype(bf)
        sc[j] = send(R.t3.at[j], R.r3.at[j], R.gssem, j, core, over_s)
    for j in (1, 3, 2):
        sib[j].wait_recv()
        tc[j].wait_recv()
        sc[j].wait_recv()
        R.t4[j - 1] = (total(j) + R.r2[j].astype(f32) + R.r3[j].astype(f32)).astype(bf)
        zc[j] = send(R.t4.at[j - 1], R.r4.at[j - 1], R.gzsem, j - 1, core, place.z(me, -j))
    sib[0].wait_recv()
    tc[0].wait_recv()
    sc[0].wait_recv()
    own = total(0) + R.r2[0].astype(f32) + R.r3[0].astype(f32)
    for j in (1, 3, 2):
        zc[j].wait_recv()
        own = own + R.r4[j - 1].astype(f32)
    R.half[core, 0] = own[:, :128]
    R.half[core, 1] = own[:, 128:]
    for group in (sib, tc, sc, zc):
        for c in group.values():
            c.wait_send()


def finish(R, place, chips):
    me, core = place.me, place.core
    loss = jnp.sum(R.loss[...], axis=1, keepdims=True)
    R.half[core, :, 201:208, :] = jnp.broadcast_to(loss, (2, 7, 128))
    both = send(R.half.at[core], R.half.at[core], R.hsem, 0, 1 - core, me)
    both.wait_recv()
    odd = lax.rem(me, 2)
    row = lax.broadcasted_iota(jnp.int32, (256, 128), 0)
    squares = jnp.zeros((1, 128), f32)
    for h in range(2):
        for lane in range(2):
            g = R.half[h, lane]
            keep = row < 201
            if h == 0:
                b_in = row >= 208 + (odd if lane == 0 else 0)
            else:
                b_in = jnp.logical_and(row >= 208, row < 208 + (33 if lane == 0 else 32 + odd))
            g = jnp.where(jnp.logical_or(keep, b_in), g, 0.0)
            squares = squares + rowsum(g * g)
    R.msg[0] = jnp.broadcast_to(jnp.sum(squares, axis=1, keepdims=True), (8, 128))
    R.msg[1] = R.half[0, 0, 200:208, :] + R.half[1, 0, 200:208, :]
    R.news[0] = R.msg[...]
    sent = []
    for d in range(1, chips):
        sent.append(send(R.msg, R.news.at[d], R.nsem, d - 1, core, lax.rem(me + d, chips)))
    for lane in range(2):
        for h in range(2):
            R.flat_a[pl.ds(402 * h + lane, 201, stride=2), :] = R.half[h, lane, 0:201, :]
            R.flat[pl.ds(8 + 96 * h + lane, 48 - 8 * h, stride=2), :] = R.half[h, lane, 208:256 - 8 * h, :]
    grad_b = jnp.where(odd == 1, R.flat[9:170, :], R.flat[8:169, :])
    for c in sent:
        c.wait_recv()
    total = R.news[0]
    for d in range(1, chips):
        total = total + R.news[d]
    norm = jnp.sqrt(total[0, 0:1, :])
    R.scalars[0:1, :] = total[1, 7:8, :]
    R.scalars[2:3, :] = norm
    clip = jnp.minimum(1.0, clip_level / (norm + 1e-06))
    for grad, p, m, v, outs in ((R.flat_a[0:804, :], R.pa, R.ma, R.va, R.outs_a), (grad_b, R.pb, R.mb, R.vb, R.outs_b)):
        g = grad * clip
        first = beta_one * m[...] + (1.0 - beta_one) * g
        second = beta_two * v[...] + (1.0 - beta_two) * g * g
        step = (first * (1.0 / (1.0 - beta_one ** STEP))) / (
            jnp.sqrt(second * (1.0 / (1.0 - beta_two ** STEP))) + adam_eps)
        old = p[...]
        new = old - learn_rate * (step + decay_rate * old)
        outs[0][...] = new
        outs[1][...] = first
        outs[2][...] = second
        outs[3][...] = new.astype(bf)
    for c in sent:
        c.wait_send()
    both.wait_send()


IN_ALL = ("img", "steps", "labels", "valid", "nidx", "table", "pa", "pb", "ma", "va", "mb", "vb")


def comm_scratch(chips):
    return dict(
        w=((chips, 2, PIECE, C), bf), flat=((184, 128), f32), piece=((2, PIECE, 128), f32),
        ga=((2, A_ROWS + 16, 128), f32), gb=((2, B_ROWS + 16, 128), f32), loss=((1, C), f32),
        r1=((chips, PIECE, C), bf), r2=((8, PIECE, C), bf), r3=((4, PIECE, C), bf), r4=((3, PIECE, C), bf),
        t2=((8, PIECE, C), bf), t3=((4, PIECE, C), bf), t4=((3, PIECE, C), bf),
        half=((2, 2, PIECE, 128), f32), flat_a=((808, 128), f32), msg=((2, 8, 128), f32), news=((chips, 2, 8, 128), f32))


def sem_counts(chips):
    return dict(zsem=3, ssem=4, tsem=8, csem=16, gcsem=16, gtsem=8, gssem=4, gzsem=3, hsem=1, nsem=chips - 1)


def whole_kernel(chips, *refs):
    R = Refs()
    refs = list(refs)
    for name in IN_ALL:
        setattr(R, name, refs.pop(0))
    R.outs_a = [refs.pop(0) for _ in range(4)]
    R.outs_b = [refs.pop(0) for _ in range(4)]
    R.scalars = refs.pop(0)
    for name in list(SCRATCH) + list(comm_scratch(chips)):
        setattr(R, name, refs.pop(0))
    for name in sem_counts(chips):
        setattr(R, name, (refs.pop(0), refs.pop(0)))
    place = Place(chips)
    barrier = greet(R, place, chips)
    own_piece(R, place)
    pl.semaphore_wait(barrier, chips)
    gather_weights(R, place)
    count = spread_rows(R, chips) * POS
    R.scalars[...] = jnp.zeros((8, 128), f32)
    R.scalars[1:2, :] = count
    first_setup(R)
    unpack_weights(R, R.ga, R.gb)
    time_forward(R)
    forward_a(R)
    forward_b(R)
    head(R, 2.0 / jnp.concatenate([count, count], axis=1))
    backward_b(R)
    backward_a(R)
    st(R.ga, A_ROWS - 1, jnp.zeros((1, C), f32))
    pack_gradients(R, chips)
    reduce_gradients(R, place)
    finish(R, place, chips)


def whole_step(chips, images, timesteps, labels, valid_slot, noise_idx, noise_table,
               params_a, params_b, first_a, second_a, first_b, second_b):
    smem = pl.BlockSpec(memory_space=pltpu.SMEM)
    vmem = pl.BlockSpec(memory_space=pltpu.VMEM)
    rows = lambda v: v.reshape(-1, 128)
    shapes = [jax.ShapeDtypeStruct((n, 128), d) for n in (804, 161) for d in (f32, f32, f32, bf)]
    scratch = [pltpu.VMEM(s, d) for s, d in SCRATCH.values()] + [pltpu.VMEM(s, d) for s, d in comm_scratch(chips).values()]
    for n in sem_counts(chips).values():
        scratch += [pltpu.SemaphoreType.DMA((n,)), pltpu.SemaphoreType.DMA((n,))]
    outs = pl.pallas_call(
        functools.partial(whole_kernel, chips),
        out_shape=shapes + [jax.ShapeDtypeStruct((8, 128), f32)],
        in_specs=[vmem, smem, smem, smem] + [vmem] * 8,
        out_specs=[vmem] * 9,
        scratch_shapes=scratch,
        compiler_params=pltpu.CompilerParams(
            collective_id=0, has_side_effects=True, vmem_limit_bytes=63 * 1024 * 1024),
    )(images, timesteps, labels, valid_slot, noise_idx, noise_table, rows(params_a), rows(params_b),
      rows(first_a), rows(second_a), rows(first_b), rows(second_b))
    flat = [v.reshape(-1) for v in outs[:8]]
    return (*flat, outs[8][0, 0], outs[8][1, 0], outs[8][2, 0])


def adam_update(master, grad_in, first_mom, second, clip_scale):
    clipped = grad_in * clip_scale
    first_new = beta_one * first_mom + (1.0 - beta_one) * clipped
    second_new = beta_two * second + (1.0 - beta_two) * clipped * clipped
    first_hat = first_new / (1.0 - beta_one**STEP)
    second_hat = second_new / (1.0 - beta_two**STEP)
    master_new = master - learn_rate * (
        first_hat / (jnp.sqrt(second_hat) + adam_eps) + decay_rate * master
    )
    return (master_new, first_new, second_new)


def plain_step(images, timesteps, labels, valid_slot, noise_idx, noise_table,
               params_a, params_b, first_a, second_a, first_b, second_b):
    gather = lambda v: lax.all_gather(v.astype(bf), "fsdp", axis=0, tiled=True).reshape(-1, C)
    count = lax.psum(jnp.sum(valid_slot).astype(f32) * POS, ("dp", "fsdp"))
    ga, gb, loss = compute(images, timesteps, labels, valid_slot, (2.0 / count).reshape(1), noise_idx, noise_table,
                           gather(params_a), gather(params_b))
    flat = lambda g: jnp.concatenate([g[0], g[1]], axis=1).reshape(-1)
    shard = lambda g: lax.psum_scatter(flat(g), "fsdp", scatter_dimension=0, tiled=True)
    part_a, part_b, loss = lax.psum((shard(ga), shard(gb), jnp.sum(loss)), "dp")
    loss, squares = lax.psum((loss, jnp.sum(part_a * part_a) + jnp.sum(part_b * part_b)), "fsdp")
    norm = jnp.sqrt(squares)
    clip = jnp.minimum(1.0, clip_level / (norm + 1e-06))
    new_a = adam_update(params_a, part_a, first_a, second_a, clip)
    new_b = adam_update(params_b, part_b, first_b, second_b, clip)
    return (*new_a, new_a[0].astype(bf), *new_b, new_b[0].astype(bf), loss, count, norm)


def solution(mesh):
    chips = mesh.shape["fsdp"]
    if chips == 16 and mesh.shape["dp"] == 2:
        step = functools.partial(whole_step, chips)
    else:
        step = plain_step
    both = P(("dp", "fsdp"))
    return jax.shard_map(
        step, mesh=mesh,
        in_specs=(both, both, both, both, both, P()) + (P("fsdp"),) * 6,
        out_specs=(P("fsdp"),) * 8 + (P(),) * 3,
        check_vma=False)
```

time: 1050 us -> 142 us (0.14); the launches traced: 1030 us -> 141 us
  local copies, waits for them, and re-layouts: 311 us -> 9.52 us
  waiting for transfers between devices: 261 us -> 0 us
  blocking collectives: 187 us -> 0 us
  other arithmetic: 185 us -> 0 us
  Pallas kernels: 0 us -> 131 us
  matrix products: 65.3 us -> 0 us
  between operations: 22 us -> 0.67 us
    unnamed x4 -> x0, waiting for transfers between devices: 243 us -> none
    pallas_call x0 -> x1, Pallas kernels: none -> 131 us  [whole_step(): pl.pallas_call(functools.partial(whole_kernel, chips), out_shape=shapes +...]
    unnamed x411 -> x22, local copies, waits for them, and re-layouts: 136 us -> 8.22 us
    psum x3 -> x0, blocking collectives: 124 us -> none  [the longest x2 83.3 us: per_device(): loss_total, pixel_total = lax.psum((local_sum, local_count), ('dp', 'fsdp'))]
    scatter-add x14 -> x0, local copies, waits for them, and re-layouts: 123 us -> none  [conv_backward(): d_padded.at[:, r:r + SIDE, s:s + SIDE, :].add(d_cols[:, :, :, r * 3 + s, :])]
    all_gather x2 -> x0, other arithmetic: 75.6 us -> none  [fetch_weights(): lax.all_gather(vector.astype(jnp.bfloat16), 'fsdp', axis=0, tiled=True)]
    dot_general x32 -> x0, matrix products: 65.3 us -> none  [the longest x2 16.1 us: conv_backward(): lax.dot_general(d_low, kernel, (((1,), (1,)), ((), ())), preferred_elemen...]
    all_gather x1 -> x0, blocking collectives: 62.7 us -> none  [fetch_weights(): lax.all_gather(vector.astype(jnp.bfloat16), 'fsdp', axis=0, tiled=True)]
  transfers between devices with their start and end apart: 3 -> 0, of which waited for: 2 -> 0; matrix products, arithmetic and copies ran while one was open for 2% -> 0% of each run, Pallas kernels for 0% -> 0%
where the time goes in v1:
time: 142 us; the launch traced here: 141 us
  Pallas kernels  131 us (92%)
  local copies, waits for them, and re-layouts  9.52 us (7%)
    pallas_call x1, Pallas kernels, whole_step(): pl.pallas_call(functools.partial(whole_kernel, chips), out_shape=shapes +...  131 us
    unnamed x22, local copies, waits for them, and re-layouts  8.22 us

profile of v1, /device:TPU:0, one launch (start us, length us, event | category | flops | bytes accessed | tf_op | source)
XLA Modules:
  0.0 141.5 jit_solution(16862522602472772224)
XLA Ops:
  0.6 131.3 %shard_map.203 = (f32[804,128]{1,0:T(8,128)}, f32[804,128]{1,0:T(8,128)}, f32[804,128]{1,0:T(8,128)}, bf16[804,128]{1,0:T(8,128)(2,1)}, f32[161,128]{1,0:T(8,128...) custom-call(bf16[8,256,256]{2,1,0:T(8,128)(2,1)} %refs_0_.1, ...), custom_call_target="tpu_custom_call" | custom-call | tf_op jit(solution)/shard_map/pallas_call | solution.py:821
  131.9 1.3 fusion
  133.3 0.0 copy-start.1
  133.3 1.8 %copy.31 = f32[102912]{0:T(1024)} copy(f32[102912]{0:T(1024)} %bitcast.19) | data formatting | bytes 823296
  135.1 0.0 copy-done.1
  135.1 0.0 copy-start
  135.1 0.8 copy.32
  135.9 0.4 copy-done
  136.2 0.0 copy-start.2
  136.2 0.8 copy.33
  137.0 0.3 copy-done.2
  137.3 0.0 copy-start.5
  137.3 0.7 copy.34
  138.0 0.2 copy-done.5
  138.2 0.0 copy-start.4
  138.2 0.6 copy.35
  138.9 0.3 copy-done.4
  139.2 0.0 copy-start.3
  139.2 0.6 copy.36
  139.8 0.3 copy-done.3
  140.1 0.0 copy-start.6
  140.1 0.6 copy.37
  140.7 0.1 copy-done.6
  140.9 0.6 copy.38
Async XLA Ops:
  133.3 1.8 %copy-start.1 = (f32[804,128]{1,0:T(8,128)S(1)}, f32[804,128]{1,0:T(8,128)}, u32[]{:S(2)}) copy-start(f32[804,128]{1,0:T(8,128)} %get-tuple-element.21) | copy-start | bytes 1234948
  135.1 1.2 copy-start
  136.2 1.1 copy-start.2
  137.3 0.9 copy-start.5
  138.2 0.9 copy-start.4
  139.2 0.9 copy-start.3
  140.1 0.8 copy-start.6

commit v2 on v1

--- a/solution.py
+++ b/solution.py
@@ -21,6 +21,7 @@
 eps_norm = 1e-05
 CH = 64
 TY = 2
+U = dict(conv=8, cback=8, triple=8, attn=8, head=8, aback=8, dx3=8, chunk=8, setup=8)
 
 A_N1, A_K1, A_B1, A_W1, A_TB1, A_W2, A_TB2, A_CT, A_PT, A_PB, A_N2, A_K2, A_B2 = (
     0, 2, 2306, 2307, 2563, 2565, 3589, 3591, 3611, 4123, 4124, 4126, 6430)
@@ -80,7 +81,8 @@
         buf[pl.ds(1 + r0 // 16, y), i, :, 256 * s:256 * s + 256] = v.astype(bf).reshape(y, 16, C)
 
 
-def conv_mm(buf, kmat, y, ty=TY):
+def conv_mm(buf, kmat, y):
+    ty = TY
     parts = [buf[pl.ds(y + r, ty)].reshape(ty * 128, 3 * C) for r in range(3)]
     return dot(jnp.concatenate(parts, axis=1), kmat[...])
 
@@ -170,7 +172,7 @@
     hi, mid, lo = split3(R.table[...])
     R.tab3[...] = jnp.concatenate([hi, mid, lo], axis=1).astype(bf)
 
-    @pl.loop(0, NIMG)
+    @pl.loop(0, NIMG, unroll=U["setup"])
     def _(i):
         rows = lax.broadcasted_iota(jnp.int32, (NT, POS), 0)
         hot = jnp.where(rows == R.nidx[pl.ds(i, 1), :], 1.0, 0.0)
@@ -208,7 +210,7 @@
 
 
 def each_chunk(fn):
-    @pl.loop(0, NIMG)
+    @pl.loop(0, NIMG, unroll=U["chunk"])
     def _(i):
         for c in range(POS // CH):
             fn(i, c * CH)
@@ -218,45 +220,59 @@
     return (x - R.mean[k, pl.ds(i, 1), :]) * R.inv[k, pl.ds(i, 1), :]
 
 
-def forward_a(R):
+def step_x1(R):
     def one(i, r0):
         x = normed(R, 0, i, R.img[i, r0:r0 + CH, :].astype(f32))
         a = x * vec(R, V_G1) + vec(R, V_C1)
         put_shifts(R.buf1, i, r0, a * sigm(a))
     each_chunk(one)
 
-    @pl.loop(0, SIDE // TY)
+
+def step_conv1(R):
+    @pl.loop(0, SIDE // TY, unroll=U["conv"])
     def _(t):
         acc = conv_mm(R.buf1, R.k1, t * TY).reshape(TY, NIMG, 16, C)
         for yy in range(TY):
             R.c1[:, pl.ds(pl.multiple_of((t * TY + yy) * 16, 16), 16), :] = acc[yy] + R.addb[...]
+
+
+def step_stats1(R):
     stats(R, 1, lambda i: R.c1[i])
 
+
+def step_x2(R):
     def two(i, r0):
         x = normed(R, 1, i, R.c1[i, r0:r0 + CH, :])
         a = x * vec(R, V_G2) + vec(R, V_C2)
         put_shifts(R.buf2, i, r0, a * sigm(a))
     each_chunk(two)
 
-    @pl.loop(0, SIDE // TY)
+
+def step_conv2(R):
+    @pl.loop(0, SIDE // TY, unroll=U["conv"])
     def _(t):
         acc = conv_mm(R.buf2, R.k2, t * TY).reshape(TY, NIMG, 16, C)
         for yy in range(TY):
             at = pl.ds(pl.multiple_of((t * TY + yy) * 16, 16), 16)
             R.h1[:, at, :] = acc[yy] + R.img[:, at, :].astype(f32) + vec(R, V_B2)
+
+
+def step_stats2(R):
     stats(R, 2, lambda i: R.h1[i])
 
 
-def forward_b(R):
+def step_triple(R):
     bias = jnp.concatenate([vec(R, V_QB), jnp.zeros((1, C), f32), vec(R, V_VB)], axis=1)
 
-    @pl.loop(0, NIMG)
+    @pl.loop(0, NIMG, unroll=U["triple"])
     def _(i):
         x = (normed(R, 2, i, R.h1[i]) * vec(R, V_G3) + vec(R, V_C3)).astype(bf)
         R.x3t[:, pl.ds(pl.multiple_of(i * POS, POS), POS)] = x.T
         R.tri[i] = (dot(x, R.wt[...]) + bias).astype(bf)
 
-    @pl.loop(0, NIMG)
+
+def step_attn(R):
+    @pl.loop(0, NIMG, unroll=U["attn"])
     def _(i):
         k = R.tri[i, :, C:2 * C]
         v = R.tri[i, :, 2 * C:]
@@ -269,14 +285,18 @@
             o = dot(p.astype(bf), v).astype(bf)
             R.o[i, at, :] = o
             R.h2[i, at, :] = R.h1[i, at, :] + dot(o, R.wo[...]) + vec(R, V_BO)
+
+
+def step_stats3(R):
     stats(R, 3, lambda i: R.h2[i])
 
 
-def head(R, scale):
+def step_head(R):
+    scale = R.scale_row[...]
     R.loss[...] = jnp.zeros_like(R.loss)
     R.sh[...] = jnp.zeros_like(R.sh)
 
-    @pl.loop(0, NIMG)
+    @pl.loop(0, NIMG, unroll=U["head"])
     def _(i):
         valid = R.valid[i].astype(f32)
         s1 = jnp.zeros((1, C), f32)
@@ -303,20 +323,19 @@
         R.s2[pl.ds(i, 1), :] = s2
 
 
-def weight_grad(R, xt, low, put):
-    put(dot(xt[...], low[...].reshape(NIMG * POS, low.shape[-1])))
-
-
-def backward_b(R):
+def step_head_grads(R):
     st(R.gb, B_BH, R.sh[...])
     st(R.gb, B_WH, dot(R.xt[...], R.low[...].reshape(NIMG * POS, C)))
     dg, db = norm_sums(R, 3, vec(R, V_G4))
     st(R.gb, B_N4, dg)
     st(R.gb, B_N4 + 1, db)
+
+
+def step_attn_back(R):
     R.sh[...] = jnp.zeros_like(R.sh)
     R.sq[...] = jnp.zeros_like(R.sq)
 
-    @pl.loop(0, NIMG)
+    @pl.loop(0, NIMG, unroll=U["aback"])
     def _(i):
         x = normed(R, 3, i, R.h2[i])
         d = (R.inv[3, pl.ds(i, 1), :] * vec(R, V_G4)) * R.da[i] - R.m1[pl.ds(i, 1), :] - x * R.m2[pl.ds(i, 1), :]
@@ -343,14 +362,22 @@
     st(R.gb, B_BO, R.sh[...])
     st(R.gb, B_QV, R.sq[:, 0:C])
     st(R.gb, B_QV + 1, R.sq[:, C:2 * C])
+
+
+def step_out_grads(R):
     st(R.gb, B_WO, dot(R.xt[...], R.low[...].reshape(NIMG * POS, C)))
 
-    @pl.loop(0, NIMG)
+
+def step_dx3(R):
+    @pl.loop(0, NIMG, unroll=U["dx3"])
     def _(i):
         da = dot(R.tri[i], R.wtt[...])
         R.da[i] = da
         R.s1[pl.ds(i, 1), :] = rowsum(da)
         R.s2[pl.ds(i, 1), :] = rowsum(da * normed(R, 2, i, R.h1[i]))
+
+
+def step_triple_grads(R):
     for h in range(3):
         st(R.gb, B_W + h, dot(
             R.x3t[...], R.tri[:, :, 256 * h:256 * h + 256].reshape(NIMG * POS, C)), 3)
@@ -360,7 +387,7 @@
 
 
 def kernel_grad(R, buf, row):
-    @pl.loop(0, SIDE // 2)
+    @pl.loop(0, SIDE // 2, unroll=8)
     def _(t):
         x = buf[pl.ds(1 + 2 * t, 2), :, :, C:2 * C].reshape(256, C)
         R.xt[:, pl.ds(pl.multiple_of(t * 256, 256), 256)] = x.T
@@ -372,7 +399,7 @@
 
 
 def conv_back(R, kt):
-    @pl.loop(0, SIDE // TY)
+    @pl.loop(0, SIDE // TY, unroll=U["cback"])
     def _(t):
         acc = conv_mm(R.dbuf, kt, t * TY).reshape(TY, NIMG, 16, C)
         for yy in range(TY):
@@ -395,7 +422,7 @@
     each_chunk(one)
 
 
-def backward_a(R):
+def step_dh1(R):
     R.sh[...] = jnp.zeros_like(R.sh)
 
     def one(i, r0):
@@ -407,12 +434,24 @@
         put_shifts(R.dbuf, i, r0, d)
     each_chunk(one)
     st(R.ga, A_B2, R.sh[...])
+
+
+def step_dk2(R):
     kernel_grad(R, R.buf2, A_K2)
+
+
+def step_dx2(R):
     conv_back(R, R.k2t)
+
+
+def step_da2(R):
     swish_back(R, 1, lambda i, r0: R.c1[i, r0:r0 + CH, :], V_G2, V_C2, True)
     dg, db = norm_sums(R, 1, vec(R, V_G2))
     st(R.ga, A_N2, dg)
     st(R.ga, A_N2 + 1, db)
+
+
+def step_dc1(R):
     R.tmp[...] = jnp.zeros_like(R.tmp)
 
     def two(i, r0):
@@ -423,9 +462,17 @@
         R.tmp[pl.ds(i, 1), :] += rowsum(d)
         put_shifts(R.dbuf, i, r0, d)
     each_chunk(two)
-    time_backward(R)
+
+
+def step_dk1(R):
     kernel_grad(R, R.buf1, A_K1)
+
+
+def step_dx1(R):
     conv_back(R, R.k1t)
+
+
+def step_da1(R):
     swish_back(R, 0, lambda i, r0: R.img[i, r0:r0 + CH, :].astype(f32), V_G1, V_C1, False)
     st(R.ga, A_N1, rowsum(R.s2[...]))
     st(R.ga, A_N1 + 1, rowsum(R.s1[...]))
@@ -462,6 +509,11 @@
         st(R.ga, A_W1 + h, dw1[:, 256 * h:256 * h + 256], 2)
 
 
+STEPS = [step_x1, step_conv1, step_stats1, step_x2, step_conv2, step_stats2, step_triple, step_attn, step_stats3,
+         step_head, step_head_grads, step_attn_back, step_out_grads, step_dx3, step_triple_grads, step_dh1, step_dk2,
+         step_dx2, step_da2, step_dc1, time_backward, step_dx1, step_da1, step_dk1]
+
+
 SCRATCH = dict(
     k1=((2304, C), bf), k1t=((2304, C), bf), k2=((2304, C), bf), k2t=((2304, C), bf),
     tw1=((SIN, TE), bf), tw2=((TE, TE), bf), pt=((TE, C), bf),
@@ -470,7 +522,7 @@
     gm=((C, C), bf), tab3=((NT, 3 * C), bf), target=((NIMG, POS, C), f32),
     tmp=((8, C), f32), mean=((4, 8, C), f32), inv=((4, 8, C), f32),
     s1=((8, C), f32), s2=((8, C), f32), m1=((8, C), f32), m2=((8, C), f32),
-    sh=((1, C), f32), sq=((1, 2 * C), f32),
+    sh=((1, C), f32), scale_row=((1, C), f32), sq=((1, 2 * C), f32),
     emb=((8, SIN), f32), pre=((8, TE), f32), te=((8, TE), f32), addb=((8, 16, C), f32),
     buf1=((18, 8, 16, 3 * C), bf), buf2=((18, 8, 16, 3 * C), bf), dbuf=((18, 8, 16, 3 * C), bf),
     c1=((8, POS, C), f32), h1=((8, POS, C), f32), h2=((8, POS, C), f32), da=((8, POS, C), f32), dh=((8, POS, C), f32),
@@ -492,14 +544,12 @@
     for c in range(0, A_ROWS, 402):
         st(fa, c, R.wa[c:c + 402, :].astype(f32))
     st(fb, 0, R.wb[...].astype(f32))
+    R.scale_row[...] = jnp.full((1, C), R.scale[0])
     first_setup(R)
     unpack_weights(R, fa, fb)
     time_forward(R)
-    forward_a(R)
-    forward_b(R)
-    head(R, R.scale[0])
-    backward_b(R)
-    backward_a(R)
+    for step in STEPS:
+        step(R)
 
 
 def compute(img, steps, labels, valid, scale, nidx, table, wa, wb):
@@ -597,7 +647,7 @@
             R.w[place.me, h] = jnp.concatenate([R.piece[0], R.piece[1]], axis=1).astype(bf)
 
 
-def gather_weights(R, place):
+def gather_weights(R, place, meanwhile):
     me, core = place.me, place.core
     got = place.pieces()
     put = lambda k: R.w.at[k, core]
@@ -605,6 +655,8 @@
     zc = {d: send(put(me), put(me), R.zsem, d - 1, core, place.z(me, d)) for d in (1, 3, 2)}
     sc, tc, sib = {}, {}, {}
     for j in ORDER:
+        if j == 1:
+            meanwhile()
         if j:
             zc[j].wait_recv()
         sc[j] = send(put(got[j]), put(got[j]), R.ssem, j, core, over_s)
@@ -730,9 +782,10 @@
         sent.append(send(R.msg, R.news.at[d], R.nsem, d - 1, core, lax.rem(me + d, chips)))
     for lane in range(2):
         for h in range(2):
-            R.flat_a[pl.ds(402 * h + lane, 201, stride=2), :] = R.half[h, lane, 0:201, :]
+            R.out_a[pl.ds(402 * h + lane, 201, stride=2), :] = R.half[h, lane, 0:201, :]
             R.flat[pl.ds(8 + 96 * h + lane, 48 - 8 * h, stride=2), :] = R.half[h, lane, 208:256 - 8 * h, :]
     grad_b = jnp.where(odd == 1, R.flat[9:170, :], R.flat[8:169, :])
+    R.out_b[...] = jnp.where(odd == 1, R.flat[9:170, :], R.flat[8:169, :])
     for c in sent:
         c.wait_recv()
     total = R.news[0]
@@ -741,25 +794,30 @@
     norm = jnp.sqrt(total[0, 0:1, :])
     R.scalars[0:1, :] = total[1, 7:8, :]
     R.scalars[2:3, :] = norm
-    clip = jnp.minimum(1.0, clip_level / (norm + 1e-06))
-    for grad, p, m, v, outs in ((R.flat_a[0:804, :], R.pa, R.ma, R.va, R.outs_a), (grad_b, R.pb, R.mb, R.vb, R.outs_b)):
-        g = grad * clip
+    for c in sent:
+        c.wait_send()
+    both.wait_send()
+
+
+def update_kernel(grad_a, grad_b, scalars, pa, pb, ma, va, mb, vb, *outs):
+    clip = jnp.minimum(1.0, clip_level / (scalars[2:3, :] + 1e-06))
+    for grad, p, m, v, out in ((grad_a, pa, ma, va, outs[:4]), (grad_b, pb, mb, vb, outs[4:8])):
+        g = grad[...] * clip
         first = beta_one * m[...] + (1.0 - beta_one) * g
         second = beta_two * v[...] + (1.0 - beta_two) * g * g
         step = (first * (1.0 / (1.0 - beta_one ** STEP))) / (
             jnp.sqrt(second * (1.0 / (1.0 - beta_two ** STEP))) + adam_eps)
         old = p[...]
         new = old - learn_rate * (step + decay_rate * old)
-        outs[0][...] = new
-        outs[1][...] = first
-        outs[2][...] = second
-        outs[3][...] = new.astype(bf)
-    for c in sent:
-        c.wait_send()
-    both.wait_send()
-
-
-IN_ALL = ("img", "steps", "labels", "valid", "nidx", "table", "pa", "pb", "ma", "va", "mb", "vb")
+        out[0][...] = new
+        out[1][...] = first
+        out[2][...] = second
+        out[3][...] = new.astype(bf)
+    for k in range(3):
+        outs[8 + k][0] = scalars[k, 0]
+
+
+IN_ALL = ("img", "steps", "labels", "valid", "nidx", "table", "pa", "pb")
 
 
 def comm_scratch(chips):
@@ -768,7 +826,7 @@
         ga=((2, A_ROWS + 16, 128), f32), gb=((2, B_ROWS + 16, 128), f32), loss=((1, C), f32),
         r1=((chips, PIECE, C), bf), r2=((8, PIECE, C), bf), r3=((4, PIECE, C), bf), r4=((3, PIECE, C), bf),
         t2=((8, PIECE, C), bf), t3=((4, PIECE, C), bf), t4=((3, PIECE, C), bf),
-        half=((2, 2, PIECE, 128), f32), flat_a=((808, 128), f32), msg=((2, 8, 128), f32), news=((chips, 2, 8, 128), f32))
+        half=((2, 2, PIECE, 128), f32), msg=((2, 8, 128), f32), news=((chips, 2, 8, 128), f32))
 
 
 def sem_counts(chips):
@@ -780,9 +838,7 @@
     refs = list(refs)
     for name in IN_ALL:
         setattr(R, name, refs.pop(0))
-    R.outs_a = [refs.pop(0) for _ in range(4)]
-    R.outs_b = [refs.pop(0) for _ in range(4)]
-    R.scalars = refs.pop(0)
+    R.out_a, R.out_b, R.scalars = refs.pop(0), refs.pop(0), refs.pop(0)
     for name in list(SCRATCH) + list(comm_scratch(chips)):
         setattr(R, name, refs.pop(0))
     for name in sem_counts(chips):
@@ -791,18 +847,15 @@
     barrier = greet(R, place, chips)
     own_piece(R, place)
     pl.semaphore_wait(barrier, chips)
-    gather_weights(R, place)
+    gather_weights(R, place, lambda: first_setup(R))
     count = spread_rows(R, chips) * POS
     R.scalars[...] = jnp.zeros((8, 128), f32)
     R.scalars[1:2, :] = count
-    first_setup(R)
     unpack_weights(R, R.ga, R.gb)
     time_forward(R)
-    forward_a(R)
-    forward_b(R)
-    head(R, 2.0 / jnp.concatenate([count, count], axis=1))
-    backward_b(R)
-    backward_a(R)
+    R.scale_row[...] = 2.0 / jnp.concatenate([count, count], axis=1)
+    for step in STEPS:
+        step(R)
     st(R.ga, A_ROWS - 1, jnp.zeros((1, C), f32))
     pack_gradients(R, chips)
     reduce_gradients(R, place)
@@ -814,22 +867,28 @@
     smem = pl.BlockSpec(memory_space=pltpu.SMEM)
     vmem = pl.BlockSpec(memory_space=pltpu.VMEM)
     rows = lambda v: v.reshape(-1, 128)
-    shapes = [jax.ShapeDtypeStruct((n, 128), d) for n in (804, 161) for d in (f32, f32, f32, bf)]
     scratch = [pltpu.VMEM(s, d) for s, d in SCRATCH.values()] + [pltpu.VMEM(s, d) for s, d in comm_scratch(chips).values()]
     for n in sem_counts(chips).values():
         scratch += [pltpu.SemaphoreType.DMA((n,)), pltpu.SemaphoreType.DMA((n,))]
-    outs = pl.pallas_call(
+    pa, pb = rows(params_a), rows(params_b)
+    grad_a, grad_b, scalars = pl.pallas_call(
         functools.partial(whole_kernel, chips),
-        out_shape=shapes + [jax.ShapeDtypeStruct((8, 128), f32)],
-        in_specs=[vmem, smem, smem, smem] + [vmem] * 8,
-        out_specs=[vmem] * 9,
+        out_shape=[jax.ShapeDtypeStruct((n, 128), f32) for n in (804, 161, 8)],
+        in_specs=[vmem, smem, smem, smem] + [vmem] * 4,
+        out_specs=[vmem] * 3,
         scratch_shapes=scratch,
         compiler_params=pltpu.CompilerParams(
             collective_id=0, has_side_effects=True, vmem_limit_bytes=63 * 1024 * 1024),
-    )(images, timesteps, labels, valid_slot, noise_idx, noise_table, rows(params_a), rows(params_b),
-      rows(first_a), rows(second_a), rows(first_b), rows(second_b))
-    flat = [v.reshape(-1) for v in outs[:8]]
-    return (*flat, outs[8][0, 0], outs[8][1, 0], outs[8][2, 0])
+    )(images, timesteps, labels, valid_slot, noise_idx, noise_table, pa, pb)
+    shapes = [jax.ShapeDtypeStruct((n, 128), d) for n in (804, 161) for d in (f32, f32, f32, bf)]
+    outs = pl.pallas_call(
+        update_kernel,
+        out_shape=shapes + [jax.ShapeDtypeStruct((1,), f32)] * 3,
+        in_specs=[vmem] * 9,
+        out_specs=[vmem] * 8 + [smem] * 3,
+        compiler_params=pltpu.CompilerParams(vmem_limit_bytes=32 * 1024 * 1024),
+    )(grad_a, grad_b, scalars, pa, pb, rows(first_a), rows(second_a), rows(first_b), rows(second_b))
+    return (*(v.reshape(-1) for v in outs[:8]), *(v.reshape(()) for v in outs[8:]))
 
 
 def adam_update(master, grad_in, first_mom, second, clip_scale):

time: 142 us -> 114 us (0.80)
  Pallas kernels: 131 us -> 107 us
  local copies, waits for them, and re-layouts: 9.52 us -> 5.33 us
    pallas_call x1 -> x2, Pallas kernels: 131 us -> 107 us  [the longest x1 105 us: whole_step(): pl.pallas_call(functools.partial(whole_kernel, chips), out_shape=[jax.Sha...]
    unnamed x22 -> x18, local copies, waits for them, and re-layouts: 8.22 us -> 5.33 us
where the time goes in v2:
time: 114 us; the launch traced here: 113 us
  Pallas kernels  107 us (94%)
  local copies, waits for them, and re-layouts  5.33 us (5%)
    pallas_call x1, Pallas kernels, whole_step(): pl.pallas_call(functools.partial(whole_kernel, chips), out_shape=[jax.Sha...  105 us
    unnamed x18, local copies, waits for them, and re-layouts  5.33 us

profile of v2, /device:TPU:0, one launch (start us, length us, event | category | flops | bytes accessed | tf_op | source)
XLA Modules:
  0.0 113.2 jit_solution(7695832304182975772)
XLA Ops:
  0.6 0.0 copy-start
  0.7 0.0 copy-start.1
  0.7 0.0 copy-start.4
  0.7 105.3 %shard_map.203 = (f32[804,128]{1,0:T(8,128)}, f32[161,128]{1,0:T(8,128)}, f32[8,128]{1,0:T(8,128)}) custom-call(bf16[8,256,256]{2,1,0:T(8,128)(2,1)} %refs_0_.1, s32[8]{0:T(128)} %refs_1_.1, s32[8]{0:T(128)} %refs_2_.1, s32[8]{0:T(128)} %refs_3_.1, s32[8,256]{1,0:T(8,128)} %refs_4_.1, f32[256,256]{1,0:T(8,128)} %refs_5_.1, f32[804,128]{1,0:T(8,128)} %bitcast.17, ...), custom_call_target="tpu_custom_call" | custom-call | tf_op jit(solution)/shard_map/pallas_call | solution.py:874
  105.9 0.0 copy-start.8
  106.0 0.0 copy-done
  106.0 0.0 copy-done.1
  106.0 0.0 copy-done.4
  106.0 0.6 copy-done.8
  106.6 0.0 copy-start.2
  106.6 1.0 copy-done.2
  107.6 0.0 copy-start.3
  107.6 1.0 copy-done.3
  108.6 0.0 copy-start.5
  108.6 0.9 copy-done.5
  109.5 0.0 copy-start.6
  109.5 0.9 copy-done.6
  110.4 0.0 copy-start.7
  110.4 0.9 copy-done.7
  111.3 1.7 %shard_map.204 = (f32[804,128]{1,0:T(8,128)}, f32[804,128]{1,0:T(8,128)}, f32[804,128]{1,0:T(8,128)}, bf16[804,128]{1,0:T(8,128)(2,1)}, f32[161,128]{1,0:T(8,128...) custom-call(f32[804,128]{1,0:T(8,128)S(1)} %copy-done.3, ...), custom_call_target="tpu_custom_call" | custom-call | tf_op jit(solution)/shard_map/pallas_call | solution.py:884
Async XLA Ops:
  0.6 105.3 %copy-start = (f32[102912]{0:T(1024)S(1)}, f32[102912]{0:T(1024)}, u32[]{:S(2)}) copy-start(f32[102912]{0:T(1024)} %param.18) | copy-start | bytes 1234948
  0.7 105.3 %copy-start.1 = (f32[102912]{0:T(1024)S(1)}, f32[102912]{0:T(1024)}, u32[]{:S(2)}) copy-start(f32[102912]{0:T(1024)} %param.20) | copy-start | bytes 1234948
  0.7 105.3 %copy-start.4 = (f32[20608]{0:T(1024)S(1)}, f32[20608]{0:T(1024)}, u32[]{:S(2)}) copy-start(f32[20608]{0:T(1024)} %param.19) | copy-start | bytes 247300
  105.9 0.7 copy-start.8
  106.6 1.0 copy-start.2
  107.6 1.0 copy-start.3
  108.6 0.9 copy-start.5
  109.5 0.9 copy-start.6
  110.4 0.9 copy-start.7

commit v3 on v2

--- a/solution.py
+++ b/solution.py
@@ -386,20 +386,22 @@
     st(R.gb, B_N3 + 1, db)
 
 
-def kernel_grad(R, buf, row):
+def kernel_lhs(R, buf):
     @pl.loop(0, SIDE // 2, unroll=8)
     def _(t):
         x = buf[pl.ds(1 + 2 * t, 2), :, :, C:2 * C].reshape(256, C)
         R.xt[:, pl.ds(pl.multiple_of(t * 256, 256), 256)] = x.T
-    for r in range(3):
-        for s in range(3):
-            d = R.dbuf[2 - r:18 - r, :, :, 256 * (2 - s):256 * (3 - s)].reshape(NIMG * POS, C)
-            at = row + (3 * r + s) * 256
-            st(R.ga, at, dot(R.xt[...], d))
-
-
-def conv_back(R, kt):
-    @pl.loop(0, SIDE // TY, unroll=U["cback"])
+
+
+def kernel_taps(R, row, taps):
+    for tap in taps:
+        r, s = divmod(tap, 3)
+        d = R.dbuf[2 - r:18 - r, :, :, 256 * (2 - s):256 * (3 - s)].reshape(NIMG * POS, C)
+        st(R.ga, row + tap * 256, dot(R.xt[...], d))
+
+
+def conv_back(R, kt, rows=(0, SIDE // TY)):
+    @pl.loop(rows[0], rows[1], unroll=8)
     def _(t):
         acc = conv_mm(R.dbuf, kt, t * TY).reshape(TY, NIMG, 16, C)
         for yy in range(TY):
@@ -437,11 +439,16 @@
 
 
 def step_dk2(R):
-    kernel_grad(R, R.buf2, A_K2)
-
-
-def step_dx2(R):
-    conv_back(R, R.k2t)
+    kernel_lhs(R, R.buf2)
+    kernel_taps(R, A_K2, range(9))
+
+
+def step_dx2_high(R):
+    conv_back(R, R.k2t, (0, 4))
+
+
+def step_dx2_low(R):
+    conv_back(R, R.k2t, (4, 8))
 
 
 def step_da2(R):
@@ -464,18 +471,31 @@
     each_chunk(two)
 
 
-def step_dk1(R):
-    kernel_grad(R, R.buf1, A_K1)
-
-
-def step_dx1(R):
-    conv_back(R, R.k1t)
+def step_dk1_high(R):
+    kernel_lhs(R, R.buf1)
+    kernel_taps(R, A_K1, (6, 7, 8))
+
+
+def step_dk1_mid(R):
+    kernel_taps(R, A_K1, (3, 4, 5))
+
+
+def step_dk1_low(R):
+    kernel_taps(R, A_K1, (0, 1, 2))
+
+
+def step_dx1_high(R):
+    conv_back(R, R.k1t, (0, 4))
+
+
+def step_dx1_low(R):
+    conv_back(R, R.k1t, (4, 8))
 
 
 def step_da1(R):
     swish_back(R, 0, lambda i, r0: R.img[i, r0:r0 + CH, :].astype(f32), V_G1, V_C1, False)
-    st(R.ga, A_N1, rowsum(R.s2[...]))
-    st(R.ga, A_N1 + 1, rowsum(R.s1[...]))
+    R.n1[0:1, :] = rowsum(R.s2[...])
+    R.n1[1:2, :] = rowsum(R.s1[...])
 
 
 def swish_slope(v):
@@ -509,9 +529,11 @@
         st(R.ga, A_W1 + h, dw1[:, 256 * h:256 * h + 256], 2)
 
 
-STEPS = [step_x1, step_conv1, step_stats1, step_x2, step_conv2, step_stats2, step_triple, step_attn, step_stats3,
-         step_head, step_head_grads, step_attn_back, step_out_grads, step_dx3, step_triple_grads, step_dh1, step_dk2,
-         step_dx2, step_da2, step_dc1, time_backward, step_dx1, step_da1, step_dk1]
+FORWARD = (step_x1, step_conv1, step_stats1, step_x2, step_conv2, step_stats2, step_triple, step_attn, step_stats3,
+           step_head, step_head_grads, step_attn_back, step_out_grads, step_dx3, step_triple_grads)
+BACKWARD = (step_dh1, step_dk2, step_dx2_high, step_dx2_low, step_da2, step_dc1, time_backward, step_dk1_high, step_dk1_mid, step_dk1_low,
+            step_dx1_high, step_dx1_low, step_da1)
+STEPS = FORWARD + BACKWARD
 
 
 SCRATCH = dict(
@@ -522,7 +544,7 @@
     gm=((C, C), bf), tab3=((NT, 3 * C), bf), target=((NIMG, POS, C), f32),
     tmp=((8, C), f32), mean=((4, 8, C), f32), inv=((4, 8, C), f32),
     s1=((8, C), f32), s2=((8, C), f32), m1=((8, C), f32), m2=((8, C), f32),
-    sh=((1, C), f32), scale_row=((1, C), f32), sq=((1, 2 * C), f32),
+    sh=((1, C), f32), scale_row=((1, C), f32), n1=((8, C), f32), sq=((1, 2 * C), f32),
     emb=((8, SIN), f32), pre=((8, TE), f32), te=((8, TE), f32), addb=((8, 16, C), f32),
     buf1=((18, 8, 16, 3 * C), bf), buf2=((18, 8, 16, 3 * C), bf), dbuf=((18, 8, 16, 3 * C), bf),
     c1=((8, POS, C), f32), h1=((8, POS, C), f32), h2=((8, POS, C), f32), da=((8, POS, C), f32), dh=((8, POS, C), f32),
@@ -550,6 +572,8 @@
     time_forward(R)
     for step in STEPS:
         step(R)
+    st(R.ga, A_N1, R.n1[0:2, :])
+    st(R.ga, A_ROWS - 1, jnp.zeros((1, C), f32))
 
 
 def compute(img, steps, labels, valid, scale, nidx, table, wa, wb):
@@ -700,59 +724,243 @@
     return count
 
 
-def pack_gradients(R, chips):
+def pack_a(R, zt):
+    for k in range(4 * zt, 4 * zt + 4):
+        for h in range(2):
+            R.w[k, h, 0:B_AT, :] = ld(R.ga, 402 * k + 201 * h, B_AT).astype(bf)
+
+
+def pack_b(R, chips):
     for k in range(chips):
         base = (161 * k) // 2
         for h in range(2):
-            R.w[k, h, 0:208, :] = ld(R.ga, 402 * k + 201 * h, 208).astype(bf)
-            R.w[k, h, 208:256, :] = ld(R.gb, base + 48 * h, 48).astype(bf)
-
-
-def reduce_gradients(R, place):
-    me, core = place.me, place.core
-    got = place.pieces()
-    over_s, over_t = place.s(me), place.t(me)
-    order = [12 + j for j in ORDER] + [8 + j for j in ORDER]
-    sib = {}
-    for q in order[:4] + [4 + j for j in ORDER] + order[4:] + [1, 3, 2, 0]:
-        there = q + 4 if 4 <= q < 8 else q - 4 if 8 <= q < 12 else q
-        copy = pltpu.make_async_remote_copy(
-            src_ref=R.w.at[got[q], 1 - core], dst_ref=R.r1.at[there], send_sem=R.gcsem[0].at[q],
-            recv_sem=R.gcsem[1].at[there], device_id=(1 - core, me), device_id_type=MESH)
-        copy.start()
-        sib[there] = copy
-
-    def total(q):
-        return R.w[got[q], core].astype(f32) + R.r1[q].astype(f32)
-    tc, sc, zc = {}, {}, {}
-    for q in order:
-        sib[q].wait_recv()
-        R.t2[q - 8] = total(q).astype(bf)
-        tc[q - 8] = send(R.t2.at[q - 8], R.r2.at[q - 8], R.gtsem, q - 8, core, over_t)
-    for j in ORDER:
-        q = 4 + j
-        sib[q].wait_recv()
-        tc[q].wait_recv()
-        R.t3[j] = (total(q) + R.r2[q].astype(f32)).astype(bf)
-        sc[j] = send(R.t3.at[j], R.r3.at[j], R.gssem, j, core, over_s)
-    for j in (1, 3, 2):
-        sib[j].wait_recv()
-        tc[j].wait_recv()
-        sc[j].wait_recv()
-        R.t4[j - 1] = (total(j) + R.r2[j].astype(f32) + R.r3[j].astype(f32)).astype(bf)
-        zc[j] = send(R.t4.at[j - 1], R.r4.at[j - 1], R.gzsem, j - 1, core, place.z(me, -j))
-    sib[0].wait_recv()
-    tc[0].wait_recv()
-    sc[0].wait_recv()
-    own = total(0) + R.r2[0].astype(f32) + R.r3[0].astype(f32)
-    for j in (1, 3, 2):
-        zc[j].wait_recv()
-        own = own + R.r4[j - 1].astype(f32)
-    R.half[core, 0] = own[:, :128]
-    R.half[core, 1] = own[:, 128:]
-    for group in (sib, tc, sc, zc):
-        for c in group.values():
+            R.w[k, h, B_AT:PIECE, :] = ld(R.gb, base + HALF_B * h, HALF_B).astype(bf)
+
+
+def late(src, dst, send_sem, recv_sem, core, chip):
+    return pltpu.make_async_remote_copy(src_ref=src, dst_ref=dst, send_sem=send_sem, recv_sem=recv_sem,
+                                        device_id=(core, chip), device_id_type=MESH)
+
+
+class Reduction:
+    def __init__(self, R, place, at):
+        self.R, self.place, self.at = R, place, at
+        self.planes = (at,) if at < 4 else range(4)
+        self.rows = pl.ds(0, B_AT) if at < 4 else pl.ds(B_AT, HALF_B)
+        me, core, rows = place.me, place.core, self.rows
+        self.mine = lax.rem(me, 4)
+        self.z = lax.div(me, 4)
+        group = pl.ds(4 * at, 4) if at < 4 else pl.ds(0, 16)
+        plane = pl.ds(at, 1) if at < 4 else pl.ds(0, 4)
+        sems = lambda pair: (pair[0].at[at], pair[1].at[at])
+        self.across_core = late(R.w.at[group, 1 - core, rows], R.r1.at[group, rows], *sems(R.gcsem), 1 - core, me)
+        self.across_t = late(R.t2.at[plane, :, rows], R.r2.at[plane, :, rows], *sems(R.gtsem), core, place.t(me))
+        self.across_s = late(R.t3.at[plane, rows], R.r3.at[plane, rows], *sems(R.gssem), core, place.s(me))
+        self.along = {}
+        for zt in self.planes:
+            far, mid, near = (3, 2, 1 - zt) if zt < 2 else (0, 1, 5 - zt)
+            base = 2 * (zt if at < 4 else 4 + zt)
+            go = lambda slot, to: late(R.t4.at[zt, rows], R.r4.at[zt, slot, rows], R.gzsem[0].at[base + slot],
+                                       R.gzsem[1].at[base + slot], core, 4 * to + self.mine)
+            self.along[zt] = (far, mid, near, go(1, mid), go(1, zt), go(0, zt))
+
+    def both_cores(self, k):
+        R = self.R
+        return R.w[k, self.place.core, self.rows].astype(f32) + R.r1[k, self.rows].astype(f32)
+
+    def start(self):
+        self.across_core.start()
+
+    def step_t(self):
+        R, place = self.R, self.place
+        self.across_core.wait_recv()
+        for zt in self.planes:
+            k = place.t(4 * zt + self.mine)
+            R.t2[zt, 0, self.rows] = self.both_cores(place.s(k)).astype(bf)
+            R.t2[zt, 1, self.rows] = self.both_cores(k).astype(bf)
+        self.across_t.start()
+
+    def step_s(self):
+        R = self.R
+        self.across_t.wait_recv()
+        for zt in self.planes:
+            k = self.place.s(4 * zt + self.mine)
+            R.t3[zt, self.rows] = (self.both_cores(k) + R.r2[zt, 0, self.rows].astype(f32)).astype(bf)
+        self.across_s.start()
+
+    def step_z(self):
+        R = self.R
+        self.across_s.wait_recv()
+        for zt in self.planes:
+            far, mid, near, to_mid, mid_on, near_on = self.along[zt]
+            total = (self.both_cores(4 * zt + self.mine) + R.r2[zt, 1, self.rows].astype(f32)
+                     + R.r3[zt, self.rows].astype(f32))
+
+            @pl.when(self.z == zt)
+            def _():
+                R.half[self.place.core, 0, self.rows] = total[:, :128]
+                R.half[self.place.core, 1, self.rows] = total[:, 128:]
+
+            @pl.when(self.z != zt)
+            def _():
+                R.t4[zt, self.rows] = total.astype(bf)
+
+            @pl.when(self.z == far)
+            def _():
+                to_mid.start()
+
+            @pl.when(self.z == near)
+            def _():
+                near_on.start()
+
+    def step_mid(self):
+        R = self.R
+        for zt in self.planes:
+            far, mid, near, to_mid, mid_on, near_on = self.along[zt]
+
+            @pl.when(self.z == mid)
+            def _():
+                to_mid.wait_recv()
+                R.t4[zt, self.rows] = (R.t4[zt, self.rows].astype(f32) + R.r4[zt, 1, self.rows].astype(f32)).astype(bf)
+                mid_on.start()
+
+    def step_end(self):
+        R, core = self.R, self.place.core
+        for zt in self.planes:
+            far, mid, near, to_mid, mid_on, near_on = self.along[zt]
+
+            @pl.when(self.z == zt)
+            def _():
+                near_on.wait_recv()
+                mid_on.wait_recv()
+                more = R.r4[zt, 0, self.rows].astype(f32) + R.r4[zt, 1, self.rows].astype(f32)
+                R.half[core, 0, self.rows] += more[:, :128]
+                R.half[core, 1, self.rows] += more[:, 128:]
+
+    def drain(self):
+        for c in (self.across_core, self.across_t, self.across_s):
             c.wait_send()
+        for zt in self.planes:
+            far, mid, near, to_mid, mid_on, near_on = self.along[zt]
+
+            @pl.when(self.z == far)
+            def _():
+                to_mid.wait_send()
+
+            @pl.when(self.z == mid)
+            def _():
+                mid_on.wait_send()
+
+            @pl.when(self.z == near)
+            def _():
+                near_on.wait_send()
+
+
+class NormOne:
+    def __init__(self, R, place, chips):
+        self.R, self.me, self.core, self.chips = R, place.me, place.core, chips
+        self.cross = late(R.n1, R.n1_in.at[0], R.n1sem[0].at[0], R.n1sem[1].at[0], 1 - place.core, place.me)
+        self.home = [late(R.n1_out, R.n1_in.at[d], R.n1sem[0].at[d], R.n1sem[1].at[d], place.core,
+                          lax.rem(place.me + chips - d, chips)) for d in range(1, chips)]
+
+    def start(self):
+        @pl.when(self.core == 1)
+        def _():
+            self.cross.start()
+
+    def to_home(self):
+        R = self.R
+
+        @pl.when(self.core == 0)
+        def _():
+            self.cross.wait_recv()
+            R.n1_out[...] = R.n1[...] + R.n1_in[0]
+        for d in range(1, self.chips):
+            @pl.when(jnp.logical_and(self.core == 0, self.me == d))
+            def _():
+                self.home[d - 1].start()
+
+    def end(self):
+        R = self.R
+
+        @pl.when(jnp.logical_and(self.core == 0, self.me == 0))
+        def _():
+            total = R.n1_out[...]
+            for d in range(1, self.chips):
+                self.home[d - 1].wait_recv()
+                total = total + R.n1_in[d]
+            R.half[0, 0, 0:2, :] = total[0:2, :128]
+            R.half[0, 1, 0:2, :] = total[0:2, 128:]
+
+    def drain(self):
+        @pl.when(self.core == 1)
+        def _():
+            self.cross.wait_send()
+        for d in range(1, self.chips):
+            @pl.when(jnp.logical_and(self.core == 0, self.me == d))
+            def _():
+                self.home[d - 1].wait_send()
+
+
+def backward_and_reduce(R, place, chips):
+    r0, r1, r2, r3, rb = (Reduction(R, place, at) for at in range(5))
+    n1 = NormOne(R, place, chips)
+    R.n1[...] = jnp.zeros((8, C), f32)
+    st(R.ga, A_N1, jnp.zeros((2, C), f32))
+    st(R.ga, A_ROWS - 1, jnp.zeros((1, C), f32))
+    pack_b(R, chips)
+    rb.start()
+    step_dh1(R)
+    rb.step_t()
+    step_dk2(R)
+    pack_a(R, 3)
+    r3.start()
+    rb.step_s()
+    step_dx2_high(R)
+    r3.step_t()
+    step_dx2_low(R)
+    rb.step_z()
+    step_da2(R)
+    step_dc1(R)
+    r3.step_s()
+    time_backward(R)
+    pack_a(R, 2)
+    r2.start()
+    rb.step_mid()
+    step_dk1_high(R)
+    pack_a(R, 1)
+    r1.start()
+    r2.step_t()
+    step_dk1_mid(R)
+    r3.step_z()
+    step_dk1_low(R)
+    pack_a(R, 0)
+    r0.start()
+    r1.step_t()
+    step_dx1_high(R)
+    r0.step_t()
+    r2.step_s()
+    step_dx1_low(R)
+    r3.step_mid()
+    rb.step_end()
+    step_da1(R)
+    n1.start()
+    r1.step_s()
+    r2.step_z()
+    r0.step_s()
+    n1.to_home()
+    r1.step_z()
+    r2.step_mid()
+    r3.step_end()
+    r0.step_z()
+    r1.step_mid()
+    r0.step_mid()
+    r2.step_end()
+    r1.step_end()
+    r0.step_end()
+    n1.end()
+    for c in (rb, r3, r2, r1, r0, n1):
+        c.drain()
 
 
 def finish(R, place, chips):
@@ -782,10 +990,13 @@
         sent.append(send(R.msg, R.news.at[d], R.nsem, d - 1, core, lax.rem(me + d, chips)))
     for lane in range(2):
         for h in range(2):
-            R.out_a[pl.ds(402 * h + lane, 201, stride=2), :] = R.half[h, lane, 0:201, :]
+            R.flat_a[pl.ds(402 * h + lane, 201, stride=2), :] = R.half[h, lane, 0:201, :]
             R.flat[pl.ds(8 + 96 * h + lane, 48 - 8 * h, stride=2), :] = R.half[h, lane, 208:256 - 8 * h, :]
     grad_b = jnp.where(odd == 1, R.flat[9:170, :], R.flat[8:169, :])
-    R.out_b[...] = jnp.where(odd == 1, R.flat[9:170, :], R.flat[8:169, :])
+    R.flat_b[0:161, :] = jnp.where(odd == 1, R.flat[9:170, :], R.flat[8:169, :])
+    outs = [pltpu.make_async_copy(R.flat_a, R.out_a, R.osem.at[0]), pltpu.make_async_copy(R.flat_b, R.out_b, R.osem.at[1])]
+    for c in outs:
+        c.start()
     for c in sent:
         c.wait_recv()
     total = R.news[0]
@@ -797,24 +1008,38 @@
     for c in sent:
         c.wait_send()
     both.wait_send()
-
-
-def update_kernel(grad_a, grad_b, scalars, pa, pb, ma, va, mb, vb, *outs):
+    for c in outs:
+        c.wait()
+
+
+def update_kernel(*refs):
+    ins, scalars, outs, refs = refs[:8], refs[8], refs[9:20], refs[20:]
+    bufs, news, in_sem, out_sem = refs[:8], refs[8:16], refs[16], refs[17]
+    loads = [pltpu.make_async_copy(a, b, in_sem.at[k]) for k, (a, b) in enumerate(zip(ins, bufs))]
+    for c in loads:
+        c.start()
     clip = jnp.minimum(1.0, clip_level / (scalars[2:3, :] + 1e-06))
-    for grad, p, m, v, out in ((grad_a, pa, ma, va, outs[:4]), (grad_b, pb, mb, vb, outs[4:8])):
-        g = grad[...] * clip
+    for k in range(3):
+        outs[8 + k][0] = scalars[k, 0]
+    stores = []
+    for part, rows in ((1, 161), (0, 804)):
+        grad, p, m, v = bufs[4 * part:4 * part + 4]
+        for c in loads[4 * part:4 * part + 4]:
+            c.wait()
+        g = grad[0:rows, :] * clip
         first = beta_one * m[...] + (1.0 - beta_one) * g
         second = beta_two * v[...] + (1.0 - beta_two) * g * g
         step = (first * (1.0 / (1.0 - beta_one ** STEP))) / (
             jnp.sqrt(second * (1.0 / (1.0 - beta_two ** STEP))) + adam_eps)
         old = p[...]
         new = old - learn_rate * (step + decay_rate * old)
-        out[0][...] = new
-        out[1][...] = first
-        out[2][...] = second
-        out[3][...] = new.astype(bf)
-    for k in range(3):
-        outs[8 + k][0] = scalars[k, 0]
+        for k, value in enumerate((new, first, second, new.astype(bf))):
+            news[4 * part + k][...] = value
+            c = pltpu.make_async_copy(news[4 * part + k], outs[4 * part + k], out_sem.at[4 * part + k])
+            c.start()
+            stores.append(c)
+    for c in stores:
+        c.wait()
 
 
 IN_ALL = ("img", "steps", "labels", "valid", "nidx", "table", "pa", "pb")
@@ -824,13 +1049,14 @@
     return dict(
         w=((chips, 2, PIECE, C), bf), flat=((184, 128), f32), piece=((2, PIECE, 128), f32),
         ga=((2, A_ROWS + 16, 128), f32), gb=((2, B_ROWS + 16, 128), f32), loss=((1, C), f32),
-        r1=((chips, PIECE, C), bf), r2=((8, PIECE, C), bf), r3=((4, PIECE, C), bf), r4=((3, PIECE, C), bf),
-        t2=((8, PIECE, C), bf), t3=((4, PIECE, C), bf), t4=((3, PIECE, C), bf),
-        half=((2, 2, PIECE, 128), f32), msg=((2, 8, 128), f32), news=((chips, 2, 8, 128), f32))
+        r1=((chips, PIECE, C), bf), r2=((4, 2, PIECE, C), bf), r3=((4, PIECE, C), bf), r4=((4, 2, PIECE, C), bf),
+        t2=((4, 2, PIECE, C), bf), t3=((4, PIECE, C), bf), t4=((4, PIECE, C), bf),
+        n1_in=((chips, 8, C), f32), n1_out=((8, C), f32),
+        half=((2, 2, PIECE, 128), f32), flat_a=((808, 128), f32), flat_b=((168, 128), f32), msg=((2, 8, 128), f32), news=((chips, 2, 8, 128), f32))
 
 
 def sem_counts(chips):
-    return dict(zsem=3, ssem=4, tsem=8, csem=16, gcsem=16, gtsem=8, gssem=4, gzsem=3, hsem=1, nsem=chips - 1)
+    return dict(zsem=3, ssem=4, tsem=8, csem=16, gcsem=5, gtsem=5, gssem=5, gzsem=16, n1sem=chips, hsem=1, nsem=chips - 1)
 
 
 def whole_kernel(chips, *refs):
@@ -843,6 +1069,7 @@
         setattr(R, name, refs.pop(0))
     for name in sem_counts(chips):
         setattr(R, name, (refs.pop(0), refs.pop(0)))
+    R.osem = refs.pop(0)
     place = Place(chips)
     barrier = greet(R, place, chips)
     own_piece(R, place)
@@ -854,11 +1081,9 @@
     unpack_weights(R, R.ga, R.gb)
     time_forward(R)
     R.scale_row[...] = 2.0 / jnp.concatenate([count, count], axis=1)
-    for step in STEPS:
+    for step in FORWARD:
         step(R)
-    st(R.ga, A_ROWS - 1, jnp.zeros((1, C), f32))
-    pack_gradients(R, chips)
-    reduce_gradients(R, place)
+    backward_and_reduce(R, place, chips)
     finish(R, place, chips)
 
 
@@ -866,28 +1091,32 @@
                params_a, params_b, first_a, second_a, first_b, second_b):
     smem = pl.BlockSpec(memory_space=pltpu.SMEM)
     vmem = pl.BlockSpec(memory_space=pltpu.VMEM)
+    hbm = pl.BlockSpec(memory_space=pl.ANY)
     rows = lambda v: v.reshape(-1, 128)
     scratch = [pltpu.VMEM(s, d) for s, d in SCRATCH.values()] + [pltpu.VMEM(s, d) for s, d in comm_scratch(chips).values()]
     for n in sem_counts(chips).values():
         scratch += [pltpu.SemaphoreType.DMA((n,)), pltpu.SemaphoreType.DMA((n,))]
+    scratch.append(pltpu.SemaphoreType.DMA((2,)))
     pa, pb = rows(params_a), rows(params_b)
     grad_a, grad_b, scalars = pl.pallas_call(
         functools.partial(whole_kernel, chips),
-        out_shape=[jax.ShapeDtypeStruct((n, 128), f32) for n in (804, 161, 8)],
+        out_shape=[jax.ShapeDtypeStruct((n, 128), f32) for n in (808, 168, 8)],
         in_specs=[vmem, smem, smem, smem] + [vmem] * 4,
-        out_specs=[vmem] * 3,
+        out_specs=[hbm, hbm, vmem],
         scratch_shapes=scratch,
         compiler_params=pltpu.CompilerParams(
             collective_id=0, has_side_effects=True, vmem_limit_bytes=63 * 1024 * 1024),
     )(images, timesteps, labels, valid_slot, noise_idx, noise_table, pa, pb)
     shapes = [jax.ShapeDtypeStruct((n, 128), d) for n in (804, 161) for d in (f32, f32, f32, bf)]
+    buffers = [pltpu.VMEM((n + extra, 128), f32) for n, pad in ((804, 4), (161, 7)) for extra in (pad, 0, 0, 0)]
     outs = pl.pallas_call(
         update_kernel,
         out_shape=shapes + [jax.ShapeDtypeStruct((1,), f32)] * 3,
-        in_specs=[vmem] * 9,
-        out_specs=[vmem] * 8 + [smem] * 3,
-        compiler_params=pltpu.CompilerParams(vmem_limit_bytes=32 * 1024 * 1024),
-    )(grad_a, grad_b, scalars, pa, pb, rows(first_a), rows(second_a), rows(first_b), rows(second_b))
+        in_specs=[hbm] * 8 + [vmem],
+        out_specs=[hbm] * 8 + [smem] * 3,
+        scratch_shapes=buffers + [pltpu.VMEM(s.shape, s.dtype) for s in shapes] + [pltpu.SemaphoreType.DMA((8,))] * 2,
+        compiler_params=pltpu.CompilerParams(vmem_limit_bytes=63 * 1024 * 1024),
+    )(grad_a, pa, rows(first_a), rows(second_a), grad_b, pb, rows(first_b), rows(second_b), scalars)
     return (*(v.reshape(-1) for v in outs[:8]), *(v.reshape(()) for v in outs[8:]))
 
 

time: 114 us -> 106 us (0.930)
  local copies, waits for them, and re-layouts: 5.33 us -> 0 us
  Pallas kernels: 107 us -> 104 us
    unnamed x18 -> x0, local copies, waits for them, and re-layouts: 5.33 us -> none
    pallas_call x1, Pallas kernels: 105 us -> 100 us  [whole_step(): pl.pallas_call(functools.partial(whole_kernel, chips), out_shape=[jax.Sha...]
    pallas_call x1, Pallas kernels: 1.72 us -> 4.33 us  [whole_step(): pl.pallas_call(update_kernel, out_shape=shapes + [jax.ShapeDtypeStruct((1...]
where the time goes in v3:
time: 106 us; the launch traced here: 105 us
  Pallas kernels  104 us (98%)
    pallas_call x1, Pallas kernels, whole_step(): pl.pallas_call(functools.partial(whole_kernel, chips), out_shape=[jax.Sha...  100 us
    pallas_call x1, Pallas kernels, whole_step(): pl.pallas_call(update_kernel, out_shape=shapes + [jax.ShapeDtypeStruct((1...  4.33 us

profile of v3, /device:TPU:0, one launch (start us, length us, event | category | flops | bytes accessed | tf_op | source)
XLA Modules:
  0.0 105.3 jit_solution(4384582188378225050)
XLA Ops:
  0.6 100.1 %shard_map.203 = (f32[808,128]{1,0:T(8,128)}, f32[168,128]{1,0:T(8,128)}, f32[8,128]{1,0:T(8,128)}) custom-call(bf16[8,256,256]{2,1,0:T(8,128)(2,1)} %refs_0_.1, s32[8]{0:T(128)} %refs_1_.1, s32[8]{0:T(128)} %refs_2_.1, s32[8]{0:T(128)} %refs_3_.1, s32[8,256]{1,0:T(8,128)} %refs_4_.1, f32[256,256]{1,0:T(8,128)} %refs_5_.1, f32[804,128]{1,0:T(8,128)} %bitcast.17, ...), custom_call_target="tpu_custom_call" | custom-call | tf_op jit(solution)/shard_map/pallas_call | solution.py:1101
  100.7 4.3 %shard_map.204 = (f32[804,128]{1,0:T(8,128)}, f32[804,128]{1,0:T(8,128)}, f32[804,128]{1,0:T(8,128)}, bf16[804,128]{1,0:T(8,128)(2,1)}, f32[161,128]{1,0:T(8,128...) custom-call(f32[808,128]{1,0:T(8,128)} %get-tuple-element.25.refs_0_, ...), custom_call_target="tpu_custom_call" | custom-call | tf_op jit(solution)/shard_map/pallas_call | solution.py:1112

commit v4 on v3

--- a/solution.py
+++ b/solution.py
@@ -81,10 +81,11 @@
         buf[pl.ds(1 + r0 // 16, y), i, :, 256 * s:256 * s + 256] = v.astype(bf).reshape(y, 16, C)
 
 
-def conv_mm(buf, kmat, y):
+def conv_mm(buf, kmat, y, nt=False):
     ty = TY
     parts = [buf[pl.ds(y + r, ty)].reshape(ty * 128, 3 * C) for r in range(3)]
-    return dot(jnp.concatenate(parts, axis=1), kmat[...])
+    rows = jnp.concatenate(parts, axis=1)
+    return dot_nt(rows, kmat[...]) if nt else dot(rows, kmat[...])
 
 
 class Refs:
@@ -103,31 +104,51 @@
     f[1, at, :] = value[:, 128:]
 
 
-def unpack_weights(R, fa, fb):
-    for kmat, kt, base in ((R.k1, R.k1t, A_K1), (R.k2, R.k2t, A_K2)):
-        for t in range(9):
-            w = ld(fa, base + 256 * t, 256)
-            kmat[256 * t:256 * t + 256, :] = w.astype(bf)
-            kt[256 * (8 - t):256 * (8 - t) + 256, :] = w.T.astype(bf)
+def unpack_kernel(kmat, kt, fa, base):
+    for t in range(9):
+        w = ld(fa, base + 256 * t, 256)
+        kmat[256 * t:256 * t + 256, :] = w.astype(bf)
+        kt[:, 256 * (8 - t):256 * (8 - t) + 256] = w.astype(bf)
+
+
+def unpack_norm_one(R, fa):
+    R.vec[0:2, :] = ld(fa, A_N1, 2)
+
+
+def unpack_time(R, fa):
     for h in range(2):
         R.tw1[:, 256 * h:256 * h + 256] = ld(fa, A_W1 + h, SIN, 2).astype(bf)
         R.tw2[:, 256 * h:256 * h + 256] = ld(fa, A_W2 + h, TE, 2).astype(bf)
     R.pt[...] = ld(fa, A_PT, TE).astype(bf)
+    for k, row in enumerate((A_B1, A_TB1, A_TB1 + 1, A_TB2, A_TB2 + 1, A_PB, A_N2, A_N2 + 1)):
+        R.vec[2 + k:3 + k, :] = ld(fa, row, 1)
+    R.ct[0:20, :] = ld(fa, A_CT, 20)
+
+
+def unpack_second_kernel(R, fa):
+    unpack_kernel(R.k2, R.k2t, fa, A_K2)
+    R.vec[10:11, :] = ld(fa, A_B2, 1)
+
+
+def unpack_b(R, fb):
     for h in range(3):
         w = ld(fb, B_W + h, C, 3)
         R.wt[:, 256 * h:256 * h + 256] = w.astype(bf)
         R.wtt[256 * h:256 * h + 256, :] = w.T.astype(bf)
-    w = ld(fb, B_WO, C)
-    R.wo[...] = w.astype(bf)
-    R.wot[...] = w.T.astype(bf)
-    w = ld(fb, B_WH, C)
-    R.wh[...] = w.astype(bf)
-    R.wht[...] = w.T.astype(bf)
-    for k, row in enumerate((A_N1, A_N1 + 1, A_B1, A_TB1, A_TB1 + 1, A_TB2, A_TB2 + 1, A_PB, A_N2, A_N2 + 1, A_B2)):
-        R.vec[k:k + 1, :] = ld(fa, row, 1)
+    for base, mat, turned in ((B_WO, R.wo, R.wot), (B_WH, R.wh, R.wht)):
+        w = ld(fb, base, C)
+        mat[...] = w.astype(bf)
+        turned[...] = w.T.astype(bf)
     for k, row in enumerate((B_N3, B_N3 + 1, B_QV, B_QV + 1, B_BO, B_N4, B_N4 + 1, B_BH)):
         R.vec[11 + k:12 + k, :] = ld(fb, row, 1)
-    R.ct[0:20, :] = ld(fa, A_CT, 20)
+
+
+def unpack_weights(R, fa, fb):
+    unpack_norm_one(R, fa)
+    unpack_kernel(R.k1, R.k1t, fa, A_K1)
+    unpack_time(R, fa)
+    unpack_second_kernel(R, fa)
+    unpack_b(R, fb)
 
 
 (V_G1, V_C1, V_B1, V_TB1, V_TB1B, V_TB2, V_TB2B, V_PB, V_G2, V_C2, V_B2,
@@ -142,10 +163,10 @@
     return wide_dot(s, R.gm[...])
 
 
-def stats(R, k, load):
+def stats(R, k, load, add=None):
     for i in range(NIMG):
         R.tmp[i:i + 1, :] = rowsum(load(i))
-    mean = group_mean(R, R.tmp[0:8, :])
+    mean = group_mean(R, R.tmp[0:8, :]) if add is None else group_mean(R, R.tmp[0:8, :] + POS * add) - add
     R.mean[k] = mean
     for i in range(NIMG):
         x = load(i) - mean[i:i + 1, :]
@@ -205,8 +226,7 @@
         te = te + jnp.where(lab == j, row, 0.0)
     R.te[...] = te
     add = wide_dot(te * sigm(te), R.pt[...]) + vec(R, V_PB) + vec(R, V_B1)
-    for i in range(NIMG):
-        R.addb[i] = jnp.broadcast_to(add[i:i + 1, :], (16, C))
+    R.add[...] = add
 
 
 def each_chunk(fn):
@@ -228,16 +248,20 @@
     each_chunk(one)
 
 
-def step_conv1(R):
-    @pl.loop(0, SIDE // TY, unroll=U["conv"])
+def conv_one(R, lo, hi):
+    @pl.loop(lo, hi, unroll=hi - lo)
     def _(t):
         acc = conv_mm(R.buf1, R.k1, t * TY).reshape(TY, NIMG, 16, C)
         for yy in range(TY):
-            R.c1[:, pl.ds(pl.multiple_of((t * TY + yy) * 16, 16), 16), :] = acc[yy] + R.addb[...]
+            R.c1[:, pl.ds(pl.multiple_of((t * TY + yy) * 16, 16), 16), :] = acc[yy]
+
+
+def step_conv1(R):
+    conv_one(R, 0, SIDE // TY)
 
 
 def step_stats1(R):
-    stats(R, 1, lambda i: R.c1[i])
+    stats(R, 1, lambda i: R.c1[i], R.add[...])
 
 
 def step_x2(R):
@@ -272,19 +296,18 @@
 
 
 def step_attn(R):
-    @pl.loop(0, NIMG, unroll=U["attn"])
-    def _(i):
-        k = R.tri[i, :, C:2 * C]
-        v = R.tri[i, :, 2 * C:]
-        for h in range(2):
-            at = slice(128 * h, 128 * h + 128)
-            s = dot_nt(R.tri[i, at, 0:C], k) * C ** (-0.5)
-            e = jnp.exp(s - jnp.max(s, axis=1, keepdims=True))
-            p = e * (1.0 / jnp.sum(e, axis=1, keepdims=True))
-            R.p[i, at, :] = p
-            o = dot(p.astype(bf), v).astype(bf)
-            R.o[i, at, :] = o
-            R.h2[i, at, :] = R.h1[i, at, :] + dot(o, R.wo[...]) + vec(R, V_BO)
+    for g in range(0, NIMG, 4):
+        for i in range(g, g + 4):
+            R.p[i] = dot_nt(R.tri[i, :, 0:C], R.tri[i, :, C:2 * C])
+        for i in range(g, g + 4):
+            for r in range(0, POS, CH):
+                s = R.p[i, r:r + CH, :] * C ** (-0.5)
+                e = jnp.exp(s - jnp.max(s, axis=1, keepdims=True))
+                R.p[i, r:r + CH, :] = e * (1.0 / jnp.sum(e, axis=1, keepdims=True))
+        for i in range(g, g + 4):
+            R.o[i] = dot(R.p[i].astype(bf), R.tri[i, :, 2 * C:]).astype(bf)
+        for i in range(g, g + 4):
+            R.h2[i] = R.h1[i] + dot(R.o[i], R.wo[...]) + vec(R, V_BO)
 
 
 def step_stats3(R):
@@ -293,34 +316,42 @@
 
 def step_head(R):
     scale = R.scale_row[...]
-    R.loss[...] = jnp.zeros_like(R.loss)
-    R.sh[...] = jnp.zeros_like(R.sh)
-
-    @pl.loop(0, NIMG, unroll=U["head"])
-    def _(i):
-        valid = R.valid[i].astype(f32)
-        s1 = jnp.zeros((1, C), f32)
-        s2 = jnp.zeros((1, C), f32)
-        for h in range(2):
-            at = slice(128 * h, 128 * h + 128)
-            x = normed(R, 3, i, R.h2[i, at, :])
-            a = x * vec(R, V_G4) + vec(R, V_C4)
-            sg = sigm(a)
-            x4 = (a * sg).astype(bf)
-            R.xt[:, pl.ds(pl.multiple_of(i * POS + 128 * h, 128), 128)] = x4.T
-            differ = dot(x4, R.wh[...]) + vec(R, V_BH) - R.target[i, at, :]
-            dv = valid * differ
-            R.loss[...] += rowsum(dv * differ)
-            dp = dv * scale
-            R.sh[...] += rowsum(dp)
-            low = dp.astype(bf)
-            R.low[i, at, :] = low
-            da = dot(low, R.wht[...]) * (sg * (1.0 + a * (1.0 - sg)))
-            R.da[i, at, :] = da
-            s1 += rowsum(da)
-            s2 += rowsum(da * x)
-        R.s1[pl.ds(i, 1), :] = s1
-        R.s2[pl.ds(i, 1), :] = s2
+    loss = jnp.zeros((8, C), f32)
+    bias = jnp.zeros((8, C), f32)
+    for g in range(0, NIMG, 4):
+        for i in range(g, g + 4):
+            for r in range(0, POS, CH):
+                a = normed(R, 3, i, R.h2[i, r:r + CH, :]) * vec(R, V_G4) + vec(R, V_C4)
+                R.low[i, r:r + CH, :] = (a * sigm(a)).astype(bf)
+        for i in range(g, g + 4):
+            R.da[i] = dot(R.low[i], R.wh[...])
+            R.xt[:, i * POS:(i + 1) * POS] = R.low[i].T
+        for i in range(g, g + 4):
+            valid = R.valid[i].astype(f32)
+            for r in range(0, POS, CH):
+                differ = R.da[i, r:r + CH, :] + vec(R, V_BH) - R.target[i, r:r + CH, :]
+                dv = valid * differ
+                loss += fold(dv * differ)
+                dp = dv * scale
+                bias += fold(dp)
+                R.low[i, r:r + CH, :] = dp.astype(bf)
+        for i in range(g, g + 4):
+            R.da[i] = dot(R.low[i], R.wht[...])
+        for i in range(g, g + 4):
+            s1 = jnp.zeros((8, C), f32)
+            s2 = jnp.zeros((8, C), f32)
+            for r in range(0, POS, CH):
+                x = normed(R, 3, i, R.h2[i, r:r + CH, :])
+                a = x * vec(R, V_G4) + vec(R, V_C4)
+                sg = sigm(a)
+                da = R.da[i, r:r + CH, :] * (sg * (1.0 + a * (1.0 - sg)))
+                R.da[i, r:r + CH, :] = da
+                s1 += fold(da)
+                s2 += fold(da * x)
+            R.s1[i:i + 1, :] = rowsum(s1)
+            R.s2[i:i + 1, :] = rowsum(s2)
+    R.loss[...] = rowsum(loss)
+    R.sh[...] = rowsum(bias)
 
 
 def step_head_grads(R):
@@ -332,36 +363,42 @@
 
 
 def step_attn_back(R):
-    R.sh[...] = jnp.zeros_like(R.sh)
-    R.sq[...] = jnp.zeros_like(R.sq)
-
-    @pl.loop(0, NIMG, unroll=U["aback"])
-    def _(i):
-        x = normed(R, 3, i, R.h2[i])
-        d = (R.inv[3, pl.ds(i, 1), :] * vec(R, V_G4)) * R.da[i] - R.m1[pl.ds(i, 1), :] - x * R.m2[pl.ds(i, 1), :]
-        R.dh[i] = d
-        R.sh[...] += rowsum(d)
-        low = d.astype(bf)
-        R.low[i] = low
-        R.xt[:, pl.ds(pl.multiple_of(i * POS, POS), POS)] = R.o[i].T
-        dm = dot(low, R.wot[...]).astype(bf)
-        p = R.p[i]
-        q = R.tri[i, :, 0:C]
-        k = R.tri[i, :, C:2 * C]
-        v = R.tri[i, :, 2 * C:]
-        dv = dot_tn(p.astype(bf), dm).astype(bf)
-        dpr = dot_nt(dm, v)
-        ds = (p * (dpr - jnp.sum(dpr * p, axis=1, keepdims=True))).astype(bf)
-        dq = (dot(ds, k) * C ** (-0.5)).astype(bf)
-        dk = (dot_tn(ds, q) * C ** (-0.5)).astype(bf)
-        R.tri[i, :, 0:C] = dq
-        R.tri[i, :, C:2 * C] = dk
-        R.tri[i, :, 2 * C:] = dv
-        R.sq[:, 0:C] += rowsum(dq.astype(f32))
-        R.sq[:, C:2 * C] += rowsum(dv.astype(f32))
-    st(R.gb, B_BO, R.sh[...])
-    st(R.gb, B_QV, R.sq[:, 0:C])
-    st(R.gb, B_QV + 1, R.sq[:, C:2 * C])
+    out_bias = jnp.zeros((8, C), f32)
+    q_bias = jnp.zeros((8, C), f32)
+    v_bias = jnp.zeros((8, C), f32)
+    for g in range(0, NIMG, 4):
+        four = range(g, g + 4)
+        for i in four:
+            for r in range(0, POS, CH):
+                x = normed(R, 3, i, R.h2[i, r:r + CH, :])
+                d = ((R.inv[3, i:i + 1, :] * vec(R, V_G4)) * R.da[i, r:r + CH, :]
+                     - R.m1[i:i + 1, :] - x * R.m2[i:i + 1, :])
+                R.dh[i, r:r + CH, :] = d
+                out_bias += fold(d)
+                R.low[i, r:r + CH, :] = d.astype(bf)
+            R.xt[:, i * POS:(i + 1) * POS] = R.o[i].T
+        for i in four:
+            R.o[i] = dot(R.low[i], R.wot[...]).astype(bf)
+        for i in four:
+            R.da[i] = dot_nt(R.o[i], R.tri[i, :, 2 * C:])
+            dv = dot_tn(R.p[i].astype(bf), R.o[i]).astype(bf)
+            R.tri[i, :, 2 * C:] = dv
+            v_bias += fold(dv.astype(f32))
+        for i in four:
+            for r in range(0, POS, CH):
+                p = R.p[i, r:r + CH, :]
+                dpr = R.da[i, r:r + CH, :]
+                R.p[i, r:r + CH, :] = p * (dpr - jnp.sum(dpr * p, axis=1, keepdims=True))
+        for i in four:
+            ds = R.p[i].astype(bf)
+            dq = (dot(ds, R.tri[i, :, C:2 * C]) * C ** (-0.5)).astype(bf)
+            dk = (dot_tn(ds, R.tri[i, :, 0:C]) * C ** (-0.5)).astype(bf)
+            R.tri[i, :, 0:C] = dq
+            R.tri[i, :, C:2 * C] = dk
+            q_bias += fold(dq.astype(f32))
+    st(R.gb, B_BO, rowsum(out_bias))
+    st(R.gb, B_QV, rowsum(q_bias))
+    st(R.gb, B_QV + 1, rowsum(v_bias))
 
 
 def step_out_grads(R):
@@ -401,41 +438,46 @@
 
 
 def conv_back(R, kt, rows=(0, SIDE // TY)):
-    @pl.loop(rows[0], rows[1], unroll=8)
+    @pl.loop(rows[0], rows[1], unroll=rows[1] - rows[0])
     def _(t):
-        acc = conv_mm(R.dbuf, kt, t * TY).reshape(TY, NIMG, 16, C)
+        acc = conv_mm(R.dbuf, kt, t * TY, True).reshape(TY, NIMG, 16, C)
         for yy in range(TY):
             R.da[:, pl.ds(pl.multiple_of((t * TY + yy) * 16, 16), 16), :] = acc[yy]
 
 
+def fold(x):
+    return jnp.sum(x.reshape(x.shape[0] // 8, 8, x.shape[1]), axis=0)
+
+
 def swish_back(R, k, load, vg, vc, keep):
-    R.s1[...] = jnp.zeros_like(R.s1)
-    R.s2[...] = jnp.zeros_like(R.s2)
-
-    def one(i, r0):
-        x = normed(R, k, i, load(i, r0))
-        a = x * vec(R, vg) + vec(R, vc)
-        sg = sigm(a)
-        da = R.da[i, r0:r0 + CH, :] * (sg * (1.0 + a * (1.0 - sg)))
-        if keep:
-            R.da[i, r0:r0 + CH, :] = da
-        R.s1[pl.ds(i, 1), :] += rowsum(da)
-        R.s2[pl.ds(i, 1), :] += rowsum(da * x)
-    each_chunk(one)
+    for i in range(NIMG):
+        s1 = jnp.zeros((8, C), f32)
+        s2 = jnp.zeros((8, C), f32)
+        for r0 in range(0, POS, CH):
+            x = normed(R, k, i, load(i, r0))
+            a = x * vec(R, vg) + vec(R, vc)
+            sg = sigm(a)
+            da = R.da[i, r0:r0 + CH, :] * (sg * (1.0 + a * (1.0 - sg)))
+            if keep:
+                R.da[i, r0:r0 + CH, :] = da
+            s1 += fold(da)
+            s2 += fold(da * x)
+        R.s1[i:i + 1, :] = rowsum(s1)
+        R.s2[i:i + 1, :] = rowsum(s2)
 
 
 def step_dh1(R):
-    R.sh[...] = jnp.zeros_like(R.sh)
+    R.sums8[...] = jnp.zeros_like(R.sums8)
 
     def one(i, r0):
         at = slice(r0, r0 + CH)
         x = normed(R, 2, i, R.h1[i, at, :])
         d = (R.dh[i, at, :] + (R.inv[2, pl.ds(i, 1), :] * vec(R, V_G3)) * R.da[i, at, :]
              - R.m1[pl.ds(i, 1), :] - x * R.m2[pl.ds(i, 1), :])
-        R.sh[...] += rowsum(d)
+        R.sums8[...] += fold(d)
         put_shifts(R.dbuf, i, r0, d)
     each_chunk(one)
-    st(R.ga, A_B2, R.sh[...])
+    st(R.ga, A_B2, rowsum(R.sums8[...]))
 
 
 def step_dk2(R):
@@ -529,23 +571,23 @@
         st(R.ga, A_W1 + h, dw1[:, 256 * h:256 * h + 256], 2)
 
 
-FORWARD = (step_x1, step_conv1, step_stats1, step_x2, step_conv2, step_stats2, step_triple, step_attn, step_stats3,
-           step_head, step_head_grads, step_attn_back, step_out_grads, step_dx3, step_triple_grads)
+FORWARD_A = (step_x1, step_conv1, step_stats1, step_x2, step_conv2, step_stats2)
+FORWARD_B = (step_triple, step_attn, step_stats3, step_head, step_head_grads, step_attn_back, step_out_grads, step_dx3, step_triple_grads)
 BACKWARD = (step_dh1, step_dk2, step_dx2_high, step_dx2_low, step_da2, step_dc1, time_backward, step_dk1_high, step_dk1_mid, step_dk1_low,
             step_dx1_high, step_dx1_low, step_da1)
-STEPS = FORWARD + BACKWARD
+STEPS = FORWARD_A + FORWARD_B + BACKWARD
 
 
 SCRATCH = dict(
-    k1=((2304, C), bf), k1t=((2304, C), bf), k2=((2304, C), bf), k2t=((2304, C), bf),
+    k1=((2304, C), bf), k1t=((C, 2304), bf), k2=((2304, C), bf), k2t=((C, 2304), bf),
     tw1=((SIN, TE), bf), tw2=((TE, TE), bf), pt=((TE, C), bf),
     wt=((C, 3 * C), bf), wtt=((3 * C, C), bf), wo=((C, C), bf), wot=((C, C), bf), wh=((C, C), bf), wht=((C, C), bf),
     vec=((24, C), f32), ct=((24, C), f32),
     gm=((C, C), bf), tab3=((NT, 3 * C), bf), target=((NIMG, POS, C), f32),
     tmp=((8, C), f32), mean=((4, 8, C), f32), inv=((4, 8, C), f32),
     s1=((8, C), f32), s2=((8, C), f32), m1=((8, C), f32), m2=((8, C), f32),
-    sh=((1, C), f32), scale_row=((1, C), f32), n1=((8, C), f32), sq=((1, 2 * C), f32),
-    emb=((8, SIN), f32), pre=((8, TE), f32), te=((8, TE), f32), addb=((8, 16, C), f32),
+    sh=((1, C), f32), sums8=((8, C), f32), scale_row=((1, C), f32), n1=((8, C), f32), sq=((1, 2 * C), f32),
+    emb=((8, SIN), f32), pre=((8, TE), f32), te=((8, TE), f32), add=((8, C), f32),
     buf1=((18, 8, 16, 3 * C), bf), buf2=((18, 8, 16, 3 * C), bf), dbuf=((18, 8, 16, 3 * C), bf),
     c1=((8, POS, C), f32), h1=((8, POS, C), f32), h2=((8, POS, C), f32), da=((8, POS, C), f32), dh=((8, POS, C), f32),
     p=((8, POS, POS), f32), o=((8, POS, C), bf), low=((8, POS, C), bf),
@@ -919,8 +961,8 @@
     step_dx2_high(R)
     r3.step_t()
     step_dx2_low(R)
+    step_da2(R)
     rb.step_z()
-    step_da2(R)
     step_dc1(R)
     r3.step_s()
     time_backward(R)
@@ -932,29 +974,29 @@
     r1.start()
     r2.step_t()
     step_dk1_mid(R)
+    step_dk1_low(R)
     r3.step_z()
-    step_dk1_low(R)
     pack_a(R, 0)
     r0.start()
     r1.step_t()
+    r0.step_t()
     step_dx1_high(R)
-    r0.step_t()
+    step_dx1_low(R)
     r2.step_s()
-    step_dx1_low(R)
-    r3.step_mid()
-    rb.step_end()
+    r1.step_s()
+    r0.step_s()
     step_da1(R)
     n1.start()
-    r1.step_s()
+    r3.step_mid()
     r2.step_z()
-    r0.step_s()
+    r1.step_z()
+    r0.step_z()
     n1.to_home()
-    r1.step_z()
     r2.step_mid()
-    r3.step_end()
-    r0.step_z()
     r1.step_mid()
     r0.step_mid()
+    rb.step_end()
+    r3.step_end()
     r2.step_end()
     r1.step_end()
     r0.step_end()
@@ -1042,11 +1084,14 @@
         c.wait()
 
 
-IN_ALL = ("img", "steps", "labels", "valid", "nidx", "table", "pa", "pb")
+IN_ALL = ("steps", "labels", "valid")
+LOADED = ("pa", "pb", "img", "nidx", "table")
 
 
 def comm_scratch(chips):
     return dict(
+        pa=((804, 128), f32), pb=((161, 128), f32), img=((NIMG, POS, C), bf), nidx=((NIMG, POS), jnp.int32),
+        table=((NT, C), f32),
         w=((chips, 2, PIECE, C), bf), flat=((184, 128), f32), piece=((2, PIECE, 128), f32),
         ga=((2, A_ROWS + 16, 128), f32), gb=((2, B_ROWS + 16, 128), f32), loss=((1, C), f32),
         r1=((chips, PIECE, C), bf), r2=((4, 2, PIECE, C), bf), r3=((4, PIECE, C), bf), r4=((4, 2, PIECE, C), bf),
@@ -1064,24 +1109,36 @@
     refs = list(refs)
     for name in IN_ALL:
         setattr(R, name, refs.pop(0))
+    R.sources = [refs.pop(0) for _ in LOADED]
     R.out_a, R.out_b, R.scalars = refs.pop(0), refs.pop(0), refs.pop(0)
     for name in list(SCRATCH) + list(comm_scratch(chips)):
         setattr(R, name, refs.pop(0))
     for name in sem_counts(chips):
         setattr(R, name, (refs.pop(0), refs.pop(0)))
-    R.osem = refs.pop(0)
+    R.osem, R.isem = refs.pop(0), refs.pop(0)
     place = Place(chips)
     barrier = greet(R, place, chips)
+    R.loads = []
+    for n, (name, src) in enumerate(zip(LOADED, R.sources)):
+        R.loads.append(pltpu.make_async_copy(src, getattr(R, name), R.isem.at[n]))
+        R.loads[-1].start()
+    for c in R.loads[:2]:
+        c.wait()
     own_piece(R, place)
     pl.semaphore_wait(barrier, chips)
-    gather_weights(R, place, lambda: first_setup(R))
+
+    def meanwhile():
+        for c in R.loads[2:]:
+            c.wait()
+        first_setup(R)
+    gather_weights(R, place, meanwhile)
     count = spread_rows(R, chips) * POS
     R.scalars[...] = jnp.zeros((8, 128), f32)
     R.scalars[1:2, :] = count
     unpack_weights(R, R.ga, R.gb)
     time_forward(R)
     R.scale_row[...] = 2.0 / jnp.concatenate([count, count], axis=1)
-    for step in FORWARD:
+    for step in FORWARD_A + FORWARD_B:
         step(R)
     backward_and_reduce(R, place, chips)
     finish(R, place, chips)
@@ -1096,17 +1153,17 @@
     scratch = [pltpu.VMEM(s, d) for s, d in SCRATCH.values()] + [pltpu.VMEM(s, d) for s, d in comm_scratch(chips).values()]
     for n in sem_counts(chips).values():
         scratch += [pltpu.SemaphoreType.DMA((n,)), pltpu.SemaphoreType.DMA((n,))]
-    scratch.append(pltpu.SemaphoreType.DMA((2,)))
+    scratch += [pltpu.SemaphoreType.DMA((2,)), pltpu.SemaphoreType.DMA((5,))]
     pa, pb = rows(params_a), rows(params_b)
     grad_a, grad_b, scalars = pl.pallas_call(
         functools.partial(whole_kernel, chips),
         out_shape=[jax.ShapeDtypeStruct((n, 128), f32) for n in (808, 168, 8)],
-        in_specs=[vmem, smem, smem, smem] + [vmem] * 4,
+        in_specs=[smem] * 3 + [hbm] * 5,
         out_specs=[hbm, hbm, vmem],
         scratch_shapes=scratch,
         compiler_params=pltpu.CompilerParams(
             collective_id=0, has_side_effects=True, vmem_limit_bytes=63 * 1024 * 1024),
-    )(images, timesteps, labels, valid_slot, noise_idx, noise_table, pa, pb)
+    )(timesteps, labels, valid_slot, pa, pb, images, noise_idx, noise_table)
     shapes = [jax.ShapeDtypeStruct((n, 128), d) for n in (804, 161) for d in (f32, f32, f32, bf)]
     buffers = [pltpu.VMEM((n + extra, 128), f32) for n, pad in ((804, 4), (161, 7)) for extra in (pad, 0, 0, 0)]
     outs = pl.pallas_call(

time: 106 us -> 101 us (0.953)
  Pallas kernels: 104 us -> 99.6 us
    pallas_call x1, Pallas kernels: 100 us -> 95.3 us  [whole_step(): pl.pallas_call(functools.partial(whole_kernel, chips), out_shape=[jax.Sha...]
where the time goes in v4:
time: 101 us; the launch traced here: 100 us
  Pallas kernels  99.6 us (99%)
    pallas_call x1, Pallas kernels, whole_step(): pl.pallas_call(functools.partial(whole_kernel, chips), out_shape=[jax.Sha...  95.3 us
    pallas_call x1, Pallas kernels, whole_step(): pl.pallas_call(update_kernel, out_shape=shapes + [jax.ShapeDtypeStruct((1...  4.33 us

profile of v4, /device:TPU:0, one launch (start us, length us, event | category | flops | bytes accessed | tf_op | source)
XLA Modules:
  0.0 100.5 jit_solution(13474542160526965645)
XLA Ops:
  0.6 95.3 %shard_map.203 = (f32[808,128]{1,0:T(8,128)}, f32[168,128]{1,0:T(8,128)}, f32[8,128]{1,0:T(8,128)}) custom-call(s32[8]{0:T(128)} %refs_0_.1, s32[8]{0:T(128)} %refs_1_.1, s32[8]{0:T(128)} %refs_2_.1, f32[804,128]{1,0:T(8,128)} %bitcast.17, f32[161,128]{1,0:T(8,128)} %bitcast.21, bf16[8,256,256]{2,1,0:T(8,128)(2,1)} %refs_5_.1, s32[8,256]{1,0:T(8,128)} %refs_6_.1, ...), custom_call_target="tpu_custom_call" | custom-call | tf_op jit(solution)/shard_map/pallas_call | solution.py:1158
  96.0 4.3 %shard_map.204 = (f32[804,128]{1,0:T(8,128)}, f32[804,128]{1,0:T(8,128)}, f32[804,128]{1,0:T(8,128)}, bf16[804,128]{1,0:T(8,128)(2,1)}, f32[161,128]{1,0:T(8,128...) custom-call(f32[808,128]{1,0:T(8,128)} %get-tuple-element.25.refs_0_, ...), custom_call_target="tpu_custom_call" | custom-call | tf_op jit(solution)/shard_map/pallas_call | solution.py:1169

commit v5 on v4

--- a/solution.py
+++ b/solution.py
@@ -296,17 +296,17 @@
 
 
 def step_attn(R):
-    for g in range(0, NIMG, 4):
-        for i in range(g, g + 4):
+    for g in range(0, NIMG, 8):
+        for i in range(g, g + 8):
             R.p[i] = dot_nt(R.tri[i, :, 0:C], R.tri[i, :, C:2 * C])
-        for i in range(g, g + 4):
+        for i in range(g, g + 8):
             for r in range(0, POS, CH):
                 s = R.p[i, r:r + CH, :] * C ** (-0.5)
                 e = jnp.exp(s - jnp.max(s, axis=1, keepdims=True))
                 R.p[i, r:r + CH, :] = e * (1.0 / jnp.sum(e, axis=1, keepdims=True))
-        for i in range(g, g + 4):
+        for i in range(g, g + 8):
             R.o[i] = dot(R.p[i].astype(bf), R.tri[i, :, 2 * C:]).astype(bf)
-        for i in range(g, g + 4):
+        for i in range(g, g + 8):
             R.h2[i] = R.h1[i] + dot(R.o[i], R.wo[...]) + vec(R, V_BO)
 
 
@@ -318,15 +318,17 @@
     scale = R.scale_row[...]
     loss = jnp.zeros((8, C), f32)
     bias = jnp.zeros((8, C), f32)
-    for g in range(0, NIMG, 4):
-        for i in range(g, g + 4):
+    for g in range(0, NIMG, 8):
+        for i in range(g, g + 8):
             for r in range(0, POS, CH):
                 a = normed(R, 3, i, R.h2[i, r:r + CH, :]) * vec(R, V_G4) + vec(R, V_C4)
-                R.low[i, r:r + CH, :] = (a * sigm(a)).astype(bf)
-        for i in range(g, g + 4):
+                sg = sigm(a)
+                R.low[i, r:r + CH, :] = (a * sg).astype(bf)
+                R.dh[i, r:r + CH, :] = sg * (1.0 + a * (1.0 - sg))
+        for i in range(g, g + 8):
             R.da[i] = dot(R.low[i], R.wh[...])
             R.xt[:, i * POS:(i + 1) * POS] = R.low[i].T
-        for i in range(g, g + 4):
+        for i in range(g, g + 8):
             valid = R.valid[i].astype(f32)
             for r in range(0, POS, CH):
                 differ = R.da[i, r:r + CH, :] + vec(R, V_BH) - R.target[i, r:r + CH, :]
@@ -335,16 +337,14 @@
                 dp = dv * scale
                 bias += fold(dp)
                 R.low[i, r:r + CH, :] = dp.astype(bf)
-        for i in range(g, g + 4):
+        for i in range(g, g + 8):
             R.da[i] = dot(R.low[i], R.wht[...])
-        for i in range(g, g + 4):
+        for i in range(g, g + 8):
             s1 = jnp.zeros((8, C), f32)
             s2 = jnp.zeros((8, C), f32)
             for r in range(0, POS, CH):
                 x = normed(R, 3, i, R.h2[i, r:r + CH, :])
-                a = x * vec(R, V_G4) + vec(R, V_C4)
-                sg = sigm(a)
-                da = R.da[i, r:r + CH, :] * (sg * (1.0 + a * (1.0 - sg)))
+                da = R.da[i, r:r + CH, :] * R.dh[i, r:r + CH, :]
                 R.da[i, r:r + CH, :] = da
                 s1 += fold(da)
                 s2 += fold(da * x)
@@ -366,9 +366,9 @@
     out_bias = jnp.zeros((8, C), f32)
     q_bias = jnp.zeros((8, C), f32)
     v_bias = jnp.zeros((8, C), f32)
-    for g in range(0, NIMG, 4):
-        four = range(g, g + 4)
-        for i in four:
+    for g in range(0, NIMG, 8):
+        images = range(g, g + 8)
+        for i in images:
             for r in range(0, POS, CH):
                 x = normed(R, 3, i, R.h2[i, r:r + CH, :])
                 d = ((R.inv[3, i:i + 1, :] * vec(R, V_G4)) * R.da[i, r:r + CH, :]
@@ -377,19 +377,19 @@
                 out_bias += fold(d)
                 R.low[i, r:r + CH, :] = d.astype(bf)
             R.xt[:, i * POS:(i + 1) * POS] = R.o[i].T
-        for i in four:
+        for i in images:
             R.o[i] = dot(R.low[i], R.wot[...]).astype(bf)
-        for i in four:
+        for i in images:
             R.da[i] = dot_nt(R.o[i], R.tri[i, :, 2 * C:])
             dv = dot_tn(R.p[i].astype(bf), R.o[i]).astype(bf)
             R.tri[i, :, 2 * C:] = dv
             v_bias += fold(dv.astype(f32))
-        for i in four:
+        for i in images:
             for r in range(0, POS, CH):
                 p = R.p[i, r:r + CH, :]
                 dpr = R.da[i, r:r + CH, :]
                 R.p[i, r:r + CH, :] = p * (dpr - jnp.sum(dpr * p, axis=1, keepdims=True))
-        for i in four:
+        for i in images:
             ds = R.p[i].astype(bf)
             dq = (dot(ds, R.tri[i, :, C:2 * C]) * C ** (-0.5)).astype(bf)
             dk = (dot_tn(ds, R.tri[i, :, 0:C]) * C ** (-0.5)).astype(bf)

time: 101 us -> 100 us (0.990)
  no operation moved by 1% of the time
where the time goes in v5:
time: 100 us; the launch traced here: 99.9 us
  Pallas kernels  99.1 us (99%)
    pallas_call x1, Pallas kernels, whole_step(): pl.pallas_call(functools.partial(whole_kernel, chips), out_shape=[jax.Sha...  94.7 us
    pallas_call x1, Pallas kernels, whole_step(): pl.pallas_call(update_kernel, out_shape=shapes + [jax.ShapeDtypeStruct((1...  4.33 us

profile of v5, /device:TPU:0, one launch (start us, length us, event | category | flops | bytes accessed | tf_op | source)
XLA Modules:
  0.0 99.9 jit_solution(14269560219738008020)
XLA Ops:
  0.6 94.7 %shard_map.203 = (f32[808,128]{1,0:T(8,128)}, f32[168,128]{1,0:T(8,128)}, f32[8,128]{1,0:T(8,128)}) custom-call(s32[8]{0:T(128)} %refs_0_.1, s32[8]{0:T(128)} %refs_1_.1, s32[8]{0:T(128)} %refs_2_.1, f32[804,128]{1,0:T(8,128)} %bitcast.17, f32[161,128]{1,0:T(8,128)} %bitcast.21, bf16[8,256,256]{2,1,0:T(8,128)(2,1)} %refs_5_.1, s32[8,256]{1,0:T(8,128)} %refs_6_.1, ...), custom_call_target="tpu_custom_call" | custom-call | tf_op jit(solution)/shard_map/pallas_call | solution.py:1158
  95.4 4.3 %shard_map.204 = (f32[804,128]{1,0:T(8,128)}, f32[804,128]{1,0:T(8,128)}, f32[804,128]{1,0:T(8,128)}, bf16[804,128]{1,0:T(8,128)(2,1)}, f32[161,128]{1,0:T(8,128...) custom-call(f32[808,128]{1,0:T(8,128)} %get-tuple-element.25.refs_0_, ...), custom_call_target="tpu_custom_call" | custom-call | tf_op jit(solution)/shard_map/pallas_call | solution.py:1169
